TPU v7x, 256 devices: a whole 4x4x8 slice. The times are simulated.
256 devices in a mesh: pipe: 2 (over core), dp: 32 (over z, x), tensor: 4 (over y).
Axes of the slice: x: 4, y: 4, z: 8, core: 2. Of those that a mesh axis runs over, the one named last changes fastest.
Arguments:
- text_embeds: bfloat16 [64, 128, 4096], P('dp', None, 'tensor'), may hold values from -10 to 10
- patches: bfloat16 [64, 64, 3200], P('dp', 'pipe'), may hold values from -6 to 6
- image_tokens: int32 [64], P('dp'), may hold values from 1 to 64, 2048 in all
- connector: bfloat16 [3200, 4096], P('dp', 'tensor'), may hold values from -0.109375 to 0.109375
- w_query: bfloat16 [2, 4096, 4096], P('pipe', 'dp', 'tensor'), may hold values from -2 to 2
- w_keyval: bfloat16 [2, 2, 4096, 1024], P('pipe', None, 'dp', 'tensor'), may hold values from -2 to 2
- w_out: bfloat16 [2, 4096, 4096], P('pipe', 'tensor', 'dp'), may hold values from -0.09375 to 0.09375
Outputs:
- final_hidden: bfloat16 [64, 128, 4096], P('dp', 'pipe', 'tensor')
Inputs may be any that keep to these rules, and one draw needn't show every extreme that they name: Sequence b holds image tokens at its first image_tokens[b] positions; some sequence reaches 64.
All inputs are finite; a program needn't handle non-finite values. No bound on the sum of `image_tokens` on one device may be relied on, other than what follows from the above.
Results may differ from a plain program's by a relative error of at most 0.01.
Values may be sent and summed in bfloat16 or wider, within the bound.
A program may use at most 128 MiB of HBM per device.

v0:
```python
import math

import jax
import jax.numpy as jnp
from jax import lax
from jax.sharding import PartitionSpec as P

HEAD = 128


def shifted(value, axis, steps):
    count = lax.axis_size(axis)
    leading, last = (max(0, -steps), min(count, count - steps))
    return lax.ppermute(value, axis, [(source, source + steps) for source in range(leading, last)])


def rotate(values, positions):
    half_size = values.shape[-1] // 2
    frequencies = 500000.0 ** (-(jnp.arange(half_size, dtype=jnp.float32) * 2.0 / values.shape[-1]))
    angles = positions.astype(jnp.float32)[:, None] * frequencies[None, :]
    cosine = jnp.cos(angles)[:, None, :]
    sine_part = jnp.sin(angles)[:, None, :]
    lower_half = values[..., :half_size]
    upper_half = values[..., half_size:]
    return jnp.concatenate(
        [
            lower_half * cosine - upper_half * sine_part,
            upper_half * cosine + lower_half * sine_part,
        ],
        axis=-1,
    )


def project_patches(patches, connector):
    values = patches.astype(jnp.float32)
    centered = values - jnp.mean(values, axis=-1, keepdims=True)
    normed = (
        centered * lax.rsqrt(jnp.mean(centered * centered, axis=-1, keepdims=True) + 1e-06)
    ).astype(jnp.bfloat16)
    return jnp.einsum("bpv,vd->bpd", normed, connector, preferred_element_type=jnp.float32).astype(
        jnp.bfloat16
    )


def attention_step(hidden, w_query, w_keyval, w_out):
    full_stream = lax.all_gather(hidden, "tensor", axis=2, tiled=True)
    batches, length = (full_stream.shape[0], full_stream.shape[1])
    values = full_stream.astype(jnp.float32)
    normed = (values * lax.rsqrt(jnp.mean(values * values, axis=-1, keepdims=True) + 1e-05)).astype(
        jnp.bfloat16
    )
    queries = jnp.einsum("bsd,dk->bsk", normed, w_query, preferred_element_type=jnp.float32)
    keyval = jnp.einsum("bsd,jdk->jbsk", normed, w_keyval, preferred_element_type=jnp.float32)
    query_heads = w_query.shape[1] // HEAD
    kv_heads_dev = w_keyval.shape[2] // HEAD
    group_size = query_heads // kv_heads_dev
    positions = jnp.arange(length)
    queries = rotate(queries.reshape(batches, length, query_heads, HEAD), positions).astype(
        jnp.bfloat16
    )
    queries = queries.reshape(batches, length, kv_heads_dev, group_size, HEAD)
    key_rows = rotate(keyval[0].reshape(batches, length, kv_heads_dev, HEAD), positions).astype(
        jnp.bfloat16
    )
    value_rows = keyval[1].reshape(batches, length, kv_heads_dev, HEAD).astype(jnp.bfloat16)
    scores = jnp.einsum(
        "bsgqe,btge->bgqst", queries, key_rows, preferred_element_type=jnp.float32
    ) / math.sqrt(HEAD)
    causal = positions[:, None] >= positions[None, :]
    scores = jnp.where(causal, scores, -1e30)
    scores = scores - jnp.max(scores, axis=-1, keepdims=True)
    weights = jnp.exp(scores)
    probabilities = (weights / jnp.sum(weights, axis=-1, keepdims=True)).astype(jnp.bfloat16)
    attended = jnp.einsum(
        "bgqst,btge->bsgqe", probabilities, value_rows, preferred_element_type=jnp.float32
    ).astype(jnp.bfloat16)
    attended = attended.reshape(batches, length, query_heads * HEAD)
    update = jnp.einsum("bsk,kd->bsd", attended, w_out, preferred_element_type=jnp.float32)
    summed_share = lax.psum_scatter(update, "tensor", scatter_dimension=2, tiled=True)
    return (hidden.astype(jnp.float32) + summed_share).astype(jnp.bfloat16)


def shards(text_embeds, patches, image_tokens, connector, w_query, w_keyval, w_out):
    connector_full, query_full, keyval_full, out_full = (
        lax.all_gather(connector, "dp", axis=0, tiled=True),
        lax.all_gather(w_query, "dp", axis=1, tiled=True),
        lax.all_gather(w_keyval, "dp", axis=2, tiled=True),
        lax.all_gather(w_out, "dp", axis=2, tiled=True),
    )
    query_full = query_full[0]
    keyval_full = keyval_full[0]
    out_full = out_full[0]
    sections = lax.axis_size("pipe")
    section_index = lax.axis_index("pipe")
    all_slots = lax.all_gather(patches, "pipe", axis=1, tiled=True)
    image_rows = project_patches(all_slots, connector_full)
    batches, length = (text_embeds.shape[0], text_embeds.shape[1])
    padded = jnp.pad(image_rows, ((0, 0), (0, length - image_rows.shape[1]), (0, 0)))
    inside = jnp.arange(length)[None, :] < image_tokens[:, None]
    opening = jnp.where(inside[:, :, None], padded, text_embeds)
    received = jnp.zeros_like(opening[0:1])
    finished = []
    tick_count = batches + sections - 1
    for moment in range(tick_count):
        if moment < batches:
            section_input = jnp.where(section_index == 0, opening[moment : moment + 1], received)
        else:
            section_input = received
        result = attention_step(section_input, query_full, keyval_full, out_full)
        if moment >= sections - 1:
            finished.append(result)
        if moment < tick_count - 1:
            received = shifted(result, "pipe", 1)
    completed = jnp.concatenate(finished, axis=0)
    wide_rows = completed.astype(jnp.float32)
    own_share = jnp.where(section_index == sections - 1, wide_rows, jnp.zeros_like(wide_rows))
    final_rows = lax.psum_scatter(
        own_share.astype(jnp.bfloat16), "pipe", scatter_dimension=1, tiled=True
    )
    return final_rows


def solution(mesh):
    placed = (
        P("dp", None, "tensor"),
        P("dp", "pipe", None),
        P("dp"),
        P("dp", "tensor"),
        P("pipe", "dp", "tensor"),
        P("pipe", None, "dp", "tensor"),
        P("pipe", "tensor", "dp"),
    )
    return jax.shard_map(
        shards, mesh=mesh, in_specs=placed, out_specs=P("dp", "pipe", "tensor"), check_vma=False
    )
```

profile of v0, /device:TPU:1, one launch (start us, length us, event | category | flops | bytes accessed | tf_op | source)
XLA Modules:
  0.0 651.7 jit_solution(10258496810069898515)
XLA Ops:
  7.3 5.5 all_gather.24
  13.4 90.8 %all-gather.21.cloned.1.call-done = bf16[32,100,1024]{2,1,0:T(8,128)(2,1)} async-done(((bf16[1,100,1024]{2,1,0:T(8,128)(2,1)}), bf16[32,100,1024]{2,1,0:T(8,128)(2,1)}) %all-gather.21.cloned.1.call-update) | async-done | bytes 6553616 | tf_op jit(solution)/shard_map/all_gather | solution.py:85
  104.2 8.4 %reshape.382 = bf16[3200,1024,1]{1,0,2:T(8,128)(2,1)} reshape(bf16[32,100,1024]{2,1,0:T(8,128)(2,1)} %all-gather.21.cloned.1.call-done) | data formatting | bytes 13107200
  112.6 4.0 convolution_convert_fusion.3
  120.0 21.0 %all-gather.9.cloned.1.call-done = bf16[1,128,4096]{2,1,0:T(8,128)(2,1)} async-done(((bf16[1,128,1024]{2,1,0:T(8,128)(2,1)}), bf16[1,128,4096]{2,1,0:T(8,128)(2,1)}) %all-gather.9.cloned.1.call-update) | async-done | bytes 1048592 | tf_op jit(solution)/shard_map/all_gather | solution.py:46
  141.0 1.5 fusion.21
  142.5 81.4 %all-gather.11.cloned.1.call-done = bf16[1,2,4096,256]{3,2,1,0:T(8,128)(2,1)} async-done(((bf16[1,2,128,256]{3,2,1,0:T(8,128)(2,1)}), bf16[1,2,4096,256]{3,2,1,0:T(8,128)(2,1)}) %all-gather.11.cloned.1.call-update) | async-done | bytes 4194320 | tf_op jit(solution)/shard_map/all_gather | solution.py:87
  223.9 3.3 fusion.37
  227.7 96.6 %all-gather.13.cloned.1.call-done = bf16[1,4096,1024]{2,1,0:T(8,128)(2,1)} async-done(((bf16[1,128,1024]{2,1,0:T(8,128)(2,1)}), bf16[1,4096,1024]{2,1,0:T(8,128)(2,1)}) %all-gather.13.cloned.1.call-update) | async-done | bytes 8388624 | tf_op jit(solution)/shard_map/all_gather | solution.py:86
  324.3 11.4 %copy.52 = bf16[1024,4096]{1,0:T(8,128)(2,1)} copy(bf16[1024,4096]{0,1:T(8,128)(2,1)} %bitcast.191) | data formatting | bytes 16777216 | tf_op jit(solution)/shard_map/bsd,dk->bsk/dot_general | solution.py:52
  335.7 6.0 convolution_bitcast_fusion.2
  342.9 82.4 %all-gather.15.cloned.1.call-done = bf16[1,1024,4096]{2,1,0:T(8,128)(2,1)} async-done(((bf16[1,1024,128]{2,1,0:T(8,128)(2,1)}), bf16[1,1024,4096]{2,1,0:T(8,128)(2,1)}) %all-gather.15.cloned.1.call-update) | async-done | bytes 8388624 | tf_op jit(solution)/shard_map/all_gather | solution.py:88
  425.3 6.0 fusion.6
  431.4 32.5 %reduce-scatter.5.cloned.1.call-done = f32[1,128,1024]{2,1,0:T(8,128)} async-done(((f32[1,128,4096]{2,1,0:T(8,128)}), f32[1,128,1024]{2,1,0:T(8,128)}) %reduce-scatter.5.cloned.1.call-update) | async-done | bytes 524304 | tf_op jit(solution)/shard_map/reduce_scatter | solution.py:79
  463.9 1.1 add_convert_fusion.2
  465.0 1.3 collective-permute-start
  466.3 2.1 collective-permute-done
  469.4 24.8 %all-gather.17.cloned.1.call-done = bf16[1,128,4096]{2,1,0:T(8,128)(2,1)} async-done(((bf16[1,128,1024]{2,1,0:T(8,128)(2,1)}), bf16[1,128,4096]{2,1,0:T(8,128)(2,1)}) %all-gather.17.cloned.1.call-update) | async-done | bytes 1048592 | tf_op jit(solution)/shard_map/all_gather | solution.py:46
  494.2 1.5 fusion.23
  495.8 3.3 fusion.40
  499.5 5.8 convolution_bitcast_fusion.1
  506.6 6.0 fusion.9
  512.7 33.6 %reduce-scatter.7.cloned.1.call-done = f32[1,128,1024]{2,1,0:T(8,128)} async-done(((f32[1,128,4096]{2,1,0:T(8,128)}), f32[1,128,1024]{2,1,0:T(8,128)}) %reduce-scatter.7.cloned.1.call-update) | async-done | bytes 524304 | tf_op jit(solution)/shard_map/reduce_scatter | solution.py:79
  547.5 1.3 collective-permute-start.1
  548.8 2.1 collective-permute-done.1
  551.7 25.0 %all-gather.19.cloned.1.call-done = bf16[1,128,4096]{2,1,0:T(8,128)(2,1)} async-done(((bf16[1,128,1024]{2,1,0:T(8,128)(2,1)}), bf16[1,128,4096]{2,1,0:T(8,128)(2,1)}) %all-gather.19.cloned.1.call-update) | async-done | bytes 1048592 | tf_op jit(solution)/shard_map/all_gather | solution.py:46
  576.6 1.5 fusion.25
  578.2 3.3 fusion.43
  581.9 5.8 convolution_bitcast_fusion
  589.0 6.1 fusion.12
  595.2 33.7 %reduce-scatter.9.cloned.1.call-done = f32[1,128,1024]{2,1,0:T(8,128)} async-done(((f32[1,128,4096]{2,1,0:T(8,128)}), f32[1,128,1024]{2,1,0:T(8,128)}) %reduce-scatter.9.cloned.1.call-update) | async-done | bytes 524304 | tf_op jit(solution)/shard_map/reduce_scatter | solution.py:79
  630.8 14.3 %reduce-scatter.11.cloned.1.call-done = bf16[2,64,1024]{2,1,0:T(8,128)(2,1)} async-done(((bf16[2,128,1024]{2,1,0:T(8,128)(2,1)}), bf16[2,64,1024]{2,1,0:T(8,128)(2,1)}) %reduce-scatter.11.cloned.1.call-update) | async-done | bytes 262160 | tf_op jit(solution)/shard_map/reduce_scatter | solution.py:117
  (98 shorter events, 14.5 us)
Async XLA Ops:
  6.5 6.8 %copy-start.7 = (s32[2]{0:T(128)S(1)}, s32[2]{0:T(128)}, u32[]{:S(2)}) copy-start(s32[2]{0:T(128)} %param.9) | copy-start | bytes 28
  6.5 97.7 %all-gather.21.cloned.1.call-start = ((), (), s32[]{:S(2)}) async-start(), calls=%async_computation.14 | async-start | bytes 7028736 | tf_op jit(solution)/shard_map/all_gather | solution.py:85
  7.3 133.7 %all-gather.9.cloned.1.call-start = ((), (), s32[]{:S(2)}) async-start(), calls=%async_computation.4 | async-start | bytes 1310720 | tf_op jit(solution)/shard_map/all_gather | solution.py:46
  112.6 4.0 copy-start.6
  117.6 106.3 %all-gather.11.cloned.1.call-start = ((), (), s32[]{:S(2)}) async-start(), calls=%async_computation.5 | async-start | bytes 4325376 | tf_op jit(solution)/shard_map/all_gather | solution.py:87
  118.3 205.9 %all-gather.13.cloned.1.call-start = ((), (), s32[]{:S(2)}) async-start(), calls=%async_computation.6 | async-start | bytes 8650752 | tf_op jit(solution)/shard_map/all_gather | solution.py:86
  118.9 306.4 %all-gather.15.cloned.1.call-start = ((), (), s32[]{:S(2)}) async-start(), calls=%async_computation.7 | async-start | bytes 8650752 | tf_op jit(solution)/shard_map/all_gather | solution.py:88
  119.5 344.4 %reduce-scatter.5.cloned.1.call-start = ((), (), s32[]{:S(2)}) async-start(), calls=%async_computation.8 | async-start | bytes 2621440 | tf_op jit(solution)/shard_map/reduce_scatter | solution.py:79
  324.3 11.4 %copy-start = (bf16[1,128,4096]{2,1,0:T(8,128)(2,1)S(1)}, bf16[1,128,4096]{2,1,0:T(8,128)(2,1)}, u32[]{:S(2)}) copy-start(bf16[1,128,4096]{2,1,0:T(8,128)(2,1)} %all-gather.9.cloned.1.call-done) | copy-start | bytes 3145732
  431.3 62.9 %all-gather.17.cloned.1.call-start = ((), (), s32[]{:S(2)}) async-start(), calls=%async_computation.9 | async-start | bytes 1310720 | tf_op jit(solution)/shard_map/all_gather | solution.py:46
  465.0 3.4 collective-permute-start
  469.2 77.2 %reduce-scatter.7.cloned.1.call-start = ((), (), s32[]{:S(2)}) async-start(), calls=%async_computation.10 | async-start | bytes 2621440 | tf_op jit(solution)/shard_map/reduce_scatter | solution.py:79
  495.8 3.7 copy-start.2
  512.6 33.7 %copy-start.3 = (bf16[1,128,1024]{2,1,0:T(8,128)(2,1)S(1)}, bf16[1,128,1024]{2,1,0:T(8,128)(2,1)}, u32[]{:S(2)}) copy-start(bf16[1,128,1024]{2,1,0:T(8,128)(2,1)} %slice_select_fusion.1) | copy-start | bytes 786436
  512.7 64.0 %all-gather.19.cloned.1.call-start = ((), (), s32[]{:S(2)}) async-start(), calls=%async_computation.11 | async-start | bytes 1310720 | tf_op jit(solution)/shard_map/all_gather | solution.py:46
  547.5 3.4 collective-permute-start.1
  550.9 0.7 copy-start.4
  551.6 77.2 %reduce-scatter.9.cloned.1.call-start = ((), (), s32[]{:S(2)}) async-start(), calls=%async_computation.12 | async-start | bytes 2621440 | tf_op jit(solution)/shard_map/reduce_scatter | solution.py:79
  578.2 3.7 copy-start.1
  595.1 33.7 %copy-start.5 = (bf16[1,128,1024]{2,1,0:T(8,128)(2,1)S(1)}, bf16[1,128,1024]{2,1,0:T(8,128)(2,1)}, u32[]{:S(2)}) copy-start(bf16[1,128,1024]{2,1,0:T(8,128)(2,1)} %copy-done.4) | copy-start | bytes 786436
  595.1 50.1 %reduce-scatter.11.cloned.1.call-start = ((), (), s32[]{:S(2)}) async-start(), calls=%async_computation.13 | async-start | bytes 786432 | tf_op jit(solution)/shard_map/reduce_scatter | solution.py:117
Sparse Core Ops, SparseCore 0:
  9.9 94.2 all-gather.20
  117.7 23.2 all-gather.8
  143.6 80.2 all-gather.10
  226.3 97.8 all-gather.12
  326.6 98.6 all-gather.14
  431.4 32.4 reduce-scatter.4
  469.3 24.8 all-gather.16
  512.8 33.5 reduce-scatter.6
  551.7 24.8 all-gather.18
  595.2 33.5 reduce-scatter.8
  631.5 13.6 reduce-scatter.10
where the time goes:
time: 653 us; the launch traced here: 652 us
  waiting for transfers between devices  543 us (83%)
  matrix products  51.4 us (8%)
  local copies, waits for them, and re-layouts  23.1 us (4%)
  between operations  13.7 us (2%)
  other arithmetic  11.9 us (2%)
    reduce_scatter x3, waiting for transfers between devices, attention_step(): lax.psum_scatter(update, 'tensor', scatter_dimension=2, tiled=True)  99.8 us
    all_gather x1, waiting for transfers between devices, shards(): lax.all_gather(w_query, 'dp', axis=1, tiled=True)  96.6 us
    all_gather x1, waiting for transfers between devices, shards(): lax.all_gather(connector, 'dp', axis=0, tiled=True)  90.8 us
    all_gather x1, waiting for transfers between devices, shards(): lax.all_gather(w_out, 'dp', axis=2, tiled=True)  82.4 us
    all_gather x1, waiting for transfers between devices, shards(): lax.all_gather(w_keyval, 'dp', axis=2, tiled=True)  81.4 us
    all_gather x3, waiting for transfers between devices, attention_step(): full_stream = lax.all_gather(hidden, 'tensor', axis=2, tiled=True)  70.8 us
    dot_general x3, matrix products, attention_step(): jnp.einsum('bsk,kd->bsd', attended, w_out, preferred_element_type=jnp.flo...  18.1 us
    dot_general x3, matrix products, attention_step(): jnp.einsum('bsd,dk->bsk', normed, w_query, preferred_element_type=jnp.flo...  17.6 us
  transfers between devices with their start and end apart: 13, of which 13 were waited for; matrix products, arithmetic and copies ran while one was open for 4% of the time, Pallas kernels for 0%

commit v1 on v0

v1 whole, which is shorter than its diff:
```python
import math

import jax
import jax.numpy as jnp
import numpy as np
from jax import lax
from jax.experimental import pallas as pl
from jax.experimental.pallas import tpu as pltpu
from jax.sharding import PartitionSpec as P

MESH = pl.DeviceIdType.MESH
BF = jnp.bfloat16
F32 = jnp.float32
NX, NY, NZ = 4, 4, 8
SCALE = 1.0 / math.sqrt(128)

RING = [
    (0, 1), (1, 1), (0, 2), (2, 1), (0, 3), (1, 2), (0, 4), (1, 3), (0, 5),
    (2, 2), (1, 4), (2, 3), (1, 5), (3, 1), (2, 4), (3, 2), (2, 5),
    (4, 1), (3, 3), (4, 2), (3, 4), (4, 3), (3, 5), (4, 4), (4, 5),
]


def remote(src, dst, send_sem, recv_sem, device):
    return pltpu.make_async_remote_copy(
        src_ref=src,
        dst_ref=dst,
        send_sem=send_sem,
        recv_sem=recv_sem,
        device_id=device,
        device_id_type=MESH,
    )


def kernel(
    text, patches, tokens, conn, wq, wkv, wo, cosine, sine, out,
    CN, WQ, WO, PNS, PN, TS, T0, IS, IR, H, QS, QR, AR, OS, OR, FS, FR,
    own_s, own_r, z_s, z_r, f_s, f_r, p_s, p_r, t_s, t_r, i_s, i_r,
    h_s, h_r, q_s, q_r, a_s, a_r, o_s, o_r, e_s, e_r,
):
    c = lax.axis_index("pipe")
    d = lax.axis_index("dp")
    y = lax.axis_index("tensor")
    z = lax.div(d, NX)
    x = lax.rem(d, NX)

    def at(core, zz, xx, yy):
        return (core, zz * NX + xx, yy)

    def xk(k):
        return lax.rem(x + k, NX)

    def yk(k):
        return lax.rem(y + k, NY)

    def zk(k):
        return lax.rem(z + k + NZ, NZ)

    barrier = pltpu.get_barrier_semaphore()
    greeted = [at(1 - c, z, xk(k), y) for k in range(4)]
    greeted += [at(c, z, xk(k), y) for k in range(1, 4)]
    greeted += [at(c, z, x, yk(k)) for k in range(1, 4)]
    greeted += [at(c, zk(1), x, y), at(c, zk(-1), x, y)]
    for device in greeted:
        pl.semaphore_signal(barrier, inc=1, device_id=device, device_id_type=MESH)
    pl.semaphore_wait(barrier, len(greeted))

    zrow = pl.multiple_of(z * 128, 128)
    WQ[c, pl.ds(zrow, 128), pl.ds(0, 1024)] = wq[0]
    WQ[c, pl.ds(zrow, 128), pl.ds(1024, 256)] = wkv[0, 0]
    WQ[c, pl.ds(zrow, 128), pl.ds(1280, 256)] = wkv[0, 1]
    WO[c, :, pl.ds(zrow, 128)] = wo[0]
    CN[z, pl.ds(0, 112)] = conn[pl.ds(0, 112)]

    def block(item, zz, part):
        if item == 0:
            start, size = ((0, 112), (0, 64), (64, 48))[part]
            return CN.at[zz, pl.ds(start, size)]
        s = (item - 1) // 2
        if item % 2 == 1:
            start, size = ((0, 128), (0, 64), (64, 64))[part]
            return WQ.at[s, pl.ds(pl.multiple_of(zz * 128 + start, 64), size)]
        start, size = ((0, 1024), (0, 512), (512, 512))[part]
        return WO.at[s, pl.ds(start, size), pl.ds(pl.multiple_of(zz * 128, 128), 128)]

    def own_copy(s, n):
        ref = block(1 + 2 * s + n, z, 0)
        return remote(ref, ref, own_s.at[n], own_r.at[n], at(1 - s, z, x, y))

    def ring_send(item, step, way):
        zz = zk(1 - step) if way == 0 else zk(step - 1)
        ref = block(item, zz, 0 if step < 4 else 1 + way)
        target = at(1, zk(1) if way == 0 else zk(-1), x, y)
        return remote(ref, ref, z_s.at[item, step - 1, way], z_r.at[item, step - 1, way], target)

    def ring_arrival(item, step, way):
        zz = zk(-step) if way == 0 else zk(step)
        ref = block(item, zz, 0 if step < 4 else 1 + way)
        return remote(ref, ref, z_s.at[item, step - 1, way], z_r.at[item, step - 1, way], at(0, z, x, y))

    def hand_over(item, index):
        step = index // 2 + 1
        zz = zk(-step) if index % 2 == 0 else zk(step)
        ref = block(item, zz, 0)
        return remote(ref, ref, f_s.at[item, index], f_r.at[item, index], at(0, z, x, y))

    def patch_copy(k):
        return remote(PNS.at[xk(k)], PN.at[x, :, c], p_s.at[k], p_r.at[x, c], at(0, z, xk(k), y))

    def patch_arrival(source, core):
        ref = PN.at[source, :, core]
        return remote(ref, ref, p_s.at[0], p_r.at[source, core], at(0, z, x, y))

    def normed_patches():
        values = patches[...].reshape(64, 3200).astype(F32)
        centered = values - jnp.sum(values, axis=-1, keepdims=True) / 3200.0
        variance = jnp.sum(centered * centered, axis=-1, keepdims=True) / 3200.0
        normed = centered * lax.rsqrt(variance + 1e-06)
        row = lax.broadcasted_iota(jnp.int32, (64, 1), 0)
        limit = jnp.where(row < 32, tokens[0], tokens[1])
        normed = jnp.where(c * 32 + lax.rem(row, 32) < limit, normed, 0.0)
        lane = lax.broadcasted_iota(jnp.int32, (64, 128), 1)
        for j in range(32):
            zz, xx = divmod(j, NX)
            base = (100 * j) // 128 * 128
            offset = 100 * j - base
            width = 128 if offset + 100 <= 128 else 256
            window = normed[:, base : base + width]
            if offset:
                window = pltpu.roll(window, width - offset, 1)
            part = jnp.where(lane < 100, window[:, :128], 0.0)
            PNS[xx, :, :, zz * 128 : (zz + 1) * 128] = part.astype(BF).reshape(2, 32, 128)

    @pl.when(c == 1)
    def _():
        own = [own_copy(1, 0), own_copy(1, 1)]
        for copy in own:
            copy.start()
        ring_send(0, 1, 0).start()
        ring_send(0, 1, 1).start()
        normed_patches()
        for k in range(4):
            patch_copy(k).start()
        for item, step in RING[1:]:
            if step > 1:
                ring_arrival(item, step - 1, 0).wait_recv()
                ring_arrival(item, step - 1, 1).wait_recv()
            elif item in (1, 2):
                own_copy(0, item - 1).wait_recv()
            if step < 5:
                ring_send(item, step, 0).start()
                ring_send(item, step, 1).start()
            if step > 1:
                for index in (6,) if step == 5 else (2 * step - 4, 2 * step - 3):
                    hand_over(item, index).start()
        for copy in own:
            copy.wait_send()
        for k in range(4):
            patch_copy(k).wait_send()
        for item in range(5):
            for step in range(1, 5):
                for way in range(2):
                    ring_send(item, step, way).wait_send()
            for index in range(7):
                hand_over(item, index).wait_send()

    def wait_item(item):
        for index in range(7):
            hand_over(item, index).wait_recv()

    def text_copy(half, k):
        target = at(0, z, xk(k), y)
        if half == 1:
            return remote(TS.at[xk(k), :, 1], H.at[0, :, 1, y, x], t_s.at[1, k], t_r.at[1, x], target)
        return remote(TS.at[xk(k), :, 0], T0.at[:, x], t_s.at[0, k], t_r.at[0, x], target)

    def text_arrival(half, k):
        ref = H.at[0, :, 1, y, xk(k)] if half == 1 else T0.at[:, xk(k)]
        return remote(ref, ref, t_s.at[half, k], t_r.at[half, xk(k)], at(1, z, x, y))

    def image_copy(k):
        return remote(IS.at[xk(k)], IR.at[x], i_s.at[k], i_r.at[x], at(0, z, xk(k), y))

    def image_arrival(k):
        ref = IR.at[xk(k)]
        return remote(ref, ref, i_s.at[k], i_r.at[xk(k)], at(1, z, x, y))

    def hidden_copy(s, b, h, k):
        ref = H.at[s, b, h, y]
        return remote(ref, ref, h_s.at[s, b, h, k], h_r.at[s, b, h, y], at(0, z, x, yk(k)))

    def hidden_arrival(s, b, h, k):
        ref = H.at[s, b, h, yk(k)]
        return remote(ref, ref, h_s.at[s, b, h, k], h_r.at[s, b, h, yk(k)], at(1, z, x, y))

    def qkv_copy(s, b, h, k):
        return remote(
            QS.at[s, b, h, xk(k)], QR.at[s, b, h, x], q_s.at[s, b, h, k], q_r.at[s, b, h, x], at(0, z, xk(k), y)
        )

    def qkv_arrival(s, b, h, k):
        ref = QR.at[s, b, h, xk(k)]
        return remote(ref, ref, q_s.at[s, b, h, k], q_r.at[s, b, h, xk(k)], at(1, z, x, y))

    def attended_copy(s, b, k):
        ref = AR.at[s, b, x]
        return remote(ref, ref, a_s.at[s, b, k], a_r.at[s, b, x], at(0, z, xk(k), y))

    def attended_arrival(s, b, k):
        ref = AR.at[s, b, xk(k)]
        return remote(ref, ref, a_s.at[s, b, k], a_r.at[s, b, xk(k)], at(1, z, x, y))

    def update_copy(s, b, k):
        return remote(OS.at[s, b, yk(k)], OR.at[s, b, y], o_s.at[s, b, k], o_r.at[s, b, y], at(0, z, x, yk(k)))

    def update_arrival(s, b, k):
        ref = OR.at[s, b, yk(k)]
        return remote(ref, ref, o_s.at[s, b, k], o_r.at[s, b, yk(k)], at(1, z, x, y))

    def final_copy(b, h, k):
        return remote(FS.at[b, h, xk(k)], FR.at[x, b], e_s.at[b, h, k], e_r.at[x, b], at(h, z, xk(k), y))

    def final_arrival(b, k):
        ref = FR.at[xk(k), b]
        return remote(ref, ref, e_s.at[b, 0, k], e_r.at[xk(k), b], at(1 - c, z, x, y))

    def send_text():
        position = lax.broadcasted_iota(jnp.int32, (128, 1), 0)
        for b in range(2):
            masked = jnp.where(position < tokens[b], jnp.zeros_like(text[b]), text[b])
            for xx in range(NX):
                for zz in range(2):
                    lanes = zz * 512 + xx * 128
                    TS[xx, b, :, :, zz * 128 : (zz + 1) * 128] = masked[:, lanes : lanes + 128].reshape(2, 64, 128)
        for b in range(2):
            H[0, b, 1, y, x] = TS[x, b, 1]
            T0[b, x] = TS[x, b, 0]
        for half in (1, 0):
            for k in range(1, 4):
                text_copy(half, k).start()

    def image_part():
        for core in range(2):
            for k in range(1 - core, 4):
                patch_arrival(xk(k), core).wait_recv()
        wait_item(0)
        rows = PN[...].reshape(512, 1024)
        for zz in range(2):
            for pair in range(2):
                lanes = zz * 512 + pair * 256
                product = jnp.dot(
                    rows, CN[:, :, lanes : lanes + 256].reshape(1024, 256), preferred_element_type=F32
                ).astype(BF)
                for n in range(2):
                    IS[2 * pair + n, :, :, :, zz * 128 : (zz + 1) * 128] = product[:, n * 128 : (n + 1) * 128].reshape(
                        4, 2, 64, 128
                    )
        for k in range(1, 4):
            image_copy(k).start()
        for k in range(1, 4):
            text_arrival(0, k).wait_recv()
        for k in range(1, 4):
            image_arrival(k).wait_recv()
        for b in range(2):
            total = IS[x, :, b].astype(F32)
            for k in range(1, 4):
                total = total + IR[xk(k), :, b].astype(F32)
            H[0, b, 0, y] = (total.astype(BF).astype(F32) + T0[b].astype(F32)).astype(BF)
            for k in range(1, 4):
                hidden_copy(0, b, 0, k).start()

    def project(s, b, h):
        squares = jnp.zeros((256, 256), F32)
        for q in range(4):
            values = H[s, b, h, q].reshape(256, 256).astype(F32)
            squares = squares + values * values
        squares = jnp.sum(squares, axis=-1, keepdims=True)
        high = squares.astype(BF).astype(F32)
        lane = lax.broadcasted_iota(jnp.int32, (256, 128), 1)
        QS[s, b, h, :, :, 1536:1664] = (
            jnp.where(lane < 64, high, squares - high).astype(BF).reshape(4, 64, 128)
        )

        def tile(n, _):
            lanes = pl.ds(pl.multiple_of(n * 256, 256), 256)
            total = jnp.zeros((256, 256), F32)
            for q in range(4):
                total = total + jnp.dot(
                    H[s, b, h, q].reshape(256, 256),
                    WQ[s, pl.ds(q * 256, 256), lanes],
                    preferred_element_type=F32,
                )
            QS[s, b, h, :, :, lanes] = total.astype(BF).reshape(4, 64, 256)
            return 0

        lax.fori_loop(0, 6, tile, 0)
        for k in range(1, 4):
            qkv_copy(s, b, h, k).start()

    def attend(s, b):
        queries = [[None] * 8, [None] * 8]
        keys = [[None] * 2, [None] * 2]
        values = [[None] * 2, [None] * 2]
        for h in range(2):
            for k in range(1, 4):
                qkv_arrival(s, b, h, k).wait_recv()

            def summed(start):
                lanes = slice(start, start + 128)
                total = QS[s, b, h, x, :, lanes].astype(F32)
                for k in range(1, 4):
                    total = total + QR[s, b, h, xk(k), :, lanes].astype(F32)
                return total

            squares = summed(1536)
            scale = lax.rsqrt((squares[:, 0:1] + squares[:, 64:65]) / 4096.0 + 1e-05)
            cos_rows = cosine[h * 64 : (h + 1) * 64]
            sin_rows = sine[h * 64 : (h + 1) * 64]

            def rotated(start):
                rows = summed(start) * scale
                return (rows * cos_rows + pltpu.roll(rows, 64, 1) * sin_rows).astype(BF)

            for j in range(8):
                queries[h][j] = rotated(j * 128)
            for g in range(2):
                keys[h][g] = rotated(1024 + g * 128)
                values[h][g] = (summed(1280 + g * 128) * scale).astype(BF)
        row = lax.rem(lax.broadcasted_iota(jnp.int32, (512, 128), 0), 128)
        column = lax.broadcasted_iota(jnp.int32, (512, 128), 1)
        for g in range(2):
            stacked = jnp.concatenate([queries[h][4 * g + j] for j in range(4) for h in range(2)], axis=0)
            key_rows = jnp.concatenate([keys[0][g], keys[1][g]], axis=0)
            value_rows = jnp.concatenate([values[0][g], values[1][g]], axis=0)
            scores = lax.dot_general(
                stacked, key_rows, (((1,), (1,)), ((), ())), preferred_element_type=F32
            )
            scores = jnp.where(row >= column, scores * SCALE, -1e30)
            weights = jnp.exp(scores - jnp.max(scores, axis=-1, keepdims=True))
            norm = jnp.sum(weights, axis=-1, keepdims=True)
            mixed = jnp.dot(weights.astype(BF), value_rows, preferred_element_type=F32) / norm
            for j in range(4):
                lanes = (4 * g + j) * 128
                AR[s, b, x, :, lanes : lanes + 128] = mixed[j * 128 : (j + 1) * 128].astype(BF)
        for k in range(1, 4):
            attended_copy(s, b, k).start()

    def update(s, b):
        for k in range(1, 4):
            attended_arrival(s, b, k).wait_recv()

        def tile(n, _):
            yd = yk(n + 1)
            lanes = pl.ds(pl.multiple_of(yd * 256, 256), 256)
            product = jnp.dot(AR[s, b].reshape(512, 1024), WO[s, :, lanes], preferred_element_type=F32)
            OS[s, b, yd] = product.astype(BF).reshape(4, 2, 64, 256)

            @pl.when(n < 3)
            def _():
                update_copy(s, b, n + 1).start()

            return 0

        lax.fori_loop(0, 4, tile, 0)

    def renew(s, b):
        for k in range(1, 4):
            update_arrival(s, b, k).wait_recv()
        for h in range(2):
            total = OS[s, b, y, :, h].astype(F32)
            for k in range(1, 4):
                total = total + OR[s, b, yk(k), :, h].astype(F32)
            fresh = (H[s, b, h, y].astype(F32) + total).astype(BF)

            @pl.when(s == 0)
            def _():
                H[1, b, h, y] = fresh
                for k in range(1, 4):
                    hidden_copy(1, b, h, k).start()

            @pl.when(s == 1)
            def _():
                FS[b, h] = fresh
                for k in range(1 - h, 4):
                    final_copy(b, h, k).start()

    @pl.when(c == 0)
    def _():
        own_copy(0, 0).start()
        own_copy(0, 1).start()
        send_text()
        for zz in range(NZ):
            CN[zz, pl.ds(112, 16)] = jnp.zeros((16, 1024), BF)
        normed_patches()
        PN[x, :, 0] = PNS[x]
        for k in range(1, 4):
            patch_copy(k).start()
        for k in range(1, 4):
            text_arrival(1, k).wait_recv()
        for b in range(2):
            for k in range(1, 4):
                hidden_copy(0, b, 1, k).start()
        image_part()

        def section(s, _):
            @pl.when(s == 0)
            def _():
                wait_item(1)

            @pl.when(s == 1)
            def _():
                own_copy(1, 0).wait_recv()
                wait_item(3)

            def unit(u, _):
                outer, inner = lax.div(u, 2), lax.rem(u, 2)
                b = jnp.where(s == 0, inner, outer)
                h = jnp.where(s == 0, 1 - outer, inner)
                for k in range(1, 4):
                    hidden_arrival(s, b, h, k).wait_recv()
                project(s, b, h)
                return 0

            def attention(b, _):
                attend(s, b)
                return 0

            def output(b, _):
                update(s, b)
                return 0

            def residual(b, _):
                renew(s, b)
                return 0

            lax.fori_loop(0, 4, unit, 0)
            lax.fori_loop(0, 2, attention, 0)

            @pl.when(s == 0)
            def _():
                wait_item(2)

            @pl.when(s == 1)
            def _():
                own_copy(1, 1).wait_recv()
                wait_item(4)

            lax.fori_loop(0, 2, output, 0)
            lax.fori_loop(0, 2, residual, 0)
            return 0

        lax.fori_loop(0, 2, section, 0)
        for b in range(2):
            FR[x, b] = FS[b, 0, x]

    for b in range(2):

        @pl.when(c == 1)
        def _():
            final_arrival(b, 0).wait_recv()

        for k in range(1, 4):
            final_arrival(b, k).wait_recv()
    for b in range(2):
        for xx in range(NX):
            for zz in range(2):
                lanes = zz * 512 + xx * 128
                out[b, :, lanes : lanes + 128] = FR[xx, b, :, zz * 128 : (zz + 1) * 128]

    @pl.when(c == 0)
    def _():
        own_copy(0, 0).wait_send()
        own_copy(0, 1).wait_send()
        for k in range(1, 4):
            patch_copy(k).wait_send()
            text_copy(0, k).wait_send()
            text_copy(1, k).wait_send()
            image_copy(k).wait_send()

        def drain(n, _):
            s, b = lax.div(n, 2), lax.rem(n, 2)
            for k in range(1, 4):
                for h in range(2):
                    hidden_copy(s, b, h, k).wait_send()
                    qkv_copy(s, b, h, k).wait_send()
                attended_copy(s, b, k).wait_send()
                update_copy(s, b, k).wait_send()
            return 0

        lax.fori_loop(0, 4, drain, 0)
        for b in range(2):
            for h in range(2):
                for k in range(1 - h, 4):
                    final_copy(b, h, k).wait_send()


def rotation_tables():
    frequencies = 500000.0 ** (-(np.arange(64, dtype=np.float32) * np.float32(2.0) / np.float32(128)))
    angles = np.arange(128, dtype=np.float32)[:, None] * frequencies.astype(np.float32)[None, :]
    cosine, sine = np.cos(angles), np.sin(angles)
    return (
        np.concatenate([cosine, cosine], axis=1).astype(np.float32),
        np.concatenate([-sine, sine], axis=1).astype(np.float32),
    )


def shards(text_embeds, patches, image_tokens, connector, w_query, w_keyval, w_out):
    cosine, sine = rotation_tables()
    padded = jnp.pad(connector, ((0, 12), (0, 0)))
    vmem = pl.BlockSpec(memory_space=pltpu.VMEM)
    dma = pltpu.SemaphoreType.DMA
    return pl.pallas_call(
        kernel,
        out_shape=jax.ShapeDtypeStruct((2, 64, 1024), BF),
        in_specs=[vmem, vmem, pl.BlockSpec(memory_space=pltpu.SMEM)] + [vmem] * 6,
        out_specs=vmem,
        scratch_shapes=[
            pltpu.VMEM((8, 128, 1024), BF),
            pltpu.VMEM((2, 1024, 1536), BF),
            pltpu.VMEM((2, 1024, 1024), BF),
            pltpu.VMEM((4, 2, 32, 1024), BF),
            pltpu.VMEM((4, 2, 2, 32, 1024), BF),
            pltpu.VMEM((4, 2, 2, 64, 256), BF),
            pltpu.VMEM((2, 4, 64, 256), BF),
            pltpu.VMEM((4, 4, 2, 64, 256), BF),
            pltpu.VMEM((4, 4, 2, 64, 256), BF),
            pltpu.VMEM((2, 2, 2, 4, 4, 64, 256), BF),
            pltpu.VMEM((2, 2, 2, 4, 64, 1664), BF),
            pltpu.VMEM((2, 2, 2, 4, 64, 1664), BF),
            pltpu.VMEM((2, 2, 4, 128, 1024), BF),
            pltpu.VMEM((2, 2, 4, 4, 2, 64, 256), BF),
            pltpu.VMEM((2, 2, 4, 4, 2, 64, 256), BF),
            pltpu.VMEM((2, 2, 4, 64, 256), BF),
            pltpu.VMEM((4, 2, 64, 256), BF),
            dma((2,)), dma((2,)),
            dma((5, 4, 2)), dma((5, 4, 2)),
            dma((5, 7)), dma((5, 7)),
            dma((4,)), dma((4, 2)),
            dma((2, 4)), dma((2, 4)),
            dma((4,)), dma((4,)),
            dma((2, 2, 2, 4)), dma((2, 2, 2, 4)),
            dma((2, 2, 2, 4)), dma((2, 2, 2, 4)),
            dma((2, 2, 4)), dma((2, 2, 4)),
            dma((2, 2, 4)), dma((2, 2, 4)),
            dma((2, 2, 4)), dma((4, 2)),
        ],
        compiler_params=pltpu.CompilerParams(
            collective_id=0, has_side_effects=True, vmem_limit_bytes=62 * 2**20
        ),
        cost_estimate=pl.CostEstimate(flops=11 * 10**9, bytes_accessed=20 * 10**6, transcendentals=10**6),
        name="decoder",
    )(text_embeds, patches, image_tokens, padded, w_query, w_keyval, w_out, cosine, sine)


def solution(mesh):
    placed = (
        P("dp", None, "tensor"),
        P("dp", "pipe", None),
        P("dp"),
        P("dp", "tensor"),
        P("pipe", "dp", "tensor"),
        P("pipe", None, "dp", "tensor"),
        P("pipe", "tensor", "dp"),
    )
    return jax.shard_map(
        shards, mesh=mesh, in_specs=placed, out_specs=P("dp", "pipe", "tensor"), check_vma=False
    )
```

time: 653 us -> 149 us (0.23)
  waiting for transfers between devices: 543 us -> 0 us
  Pallas kernels: 0 us -> 146 us
  matrix products: 51.4 us -> 0 us
  local copies, waits for them, and re-layouts: 23.1 us -> 3.31 us
  between operations: 13.7 us -> 0.01 us
  other arithmetic: 11.9 us -> 0 us
    all_gather x7 -> x0, waiting for transfers between devices: 422 us -> none  [the longest x1 96.6 us: shards(): lax.all_gather(w_query, 'dp', axis=1, tiled=True)]
    pallas_call x0 -> x1, Pallas kernels: none -> 146 us  [shards(): pl.pallas_call(kernel, out_shape=jax.ShapeDtypeStruct((2, 64, 1024), BF),...]
    reduce_scatter x4 -> x0, waiting for transfers between devices: 114 us -> none  [the longest x3 99.8 us: attention_step(): lax.psum_scatter(update, 'tensor', scatter_dimension=2, tiled=True)]
    dot_general x16 -> x0, matrix products: 51.4 us -> none  [the longest x3 18.1 us: attention_step(): jnp.einsum('bsk,kd->bsd', attended, w_out, preferred_element_type=jnp.flo...]
    dot_general x1 -> x0, local copies, waits for them, and re-layouts: 11.4 us -> none  [attention_step(): jnp.einsum('bsd,dk->bsk', normed, w_query, preferred_element_type=jnp.flo...]
    unnamed x21 -> x1, local copies, waits for them, and re-layouts: 9.53 us -> 1.67 us
  transfers between devices with their start and end apart: 13 -> 0, of which waited for: 13 -> 0; matrix products, arithmetic and copies ran while one was open for 4% -> 0% of each run, Pallas kernels for 0% -> 0%
where the time goes in v1:
time: 149 us
  Pallas kernels  146 us (98%)
  local copies, waits for them, and re-layouts  3.31 us (2%)
    pallas_call x1, Pallas kernels, shards(): pl.pallas_call(kernel, out_shape=jax.ShapeDtypeStruct((2, 64, 1024), BF),...  146 us

profile of v1, /device:TPU:1, one launch (start us, length us, event | category | flops | bytes accessed | tf_op | source)
XLA Modules:
  0.0 149.3 jit_solution(353461695890890290)
XLA Ops:
  0.0 1.6 %pad.4.conn = bf16[112,1024]{1,0:T(8,128)(2,1)} pad(bf16[100,1024]{1,0:T(8,128)(2,1)} %param.12, bf16[]{:T(256)} %constant.6.clone.1), padding=0_12x0_0 | pad | bytes 434178 | tf_op jit(solution)/shard_map/jit(_pad)/pad | solution.py:509
  1.6 146.0 %decoder.1 = bf16[2,64,1024]{2,1,0:T(8,128)(2,1)} custom-call(bf16[2,128,1024]{2,1,0:T(8,128)(2,1)} %text.1, bf16[2,32,3200]{2,1,0:T(8,128)(2,1)} %patches.1, s32[2]{0:T(128)} %tokens.1, bf16[112,1024]{1,0:T(8,128)(2,1)} %pad.4.conn, bf16[1,128,1024]{2,1,0:T(8,128)(2,1)} %wq.1, bf16[1,2,128,256]{3,2,1,0:T(8,128)(2,1)} %wkv.1, bf16[1,1024,128]{2,1,0:T(8,128)(2,1)} %wo.1, ...), custom_call_target="tpu_custom_call" | custom-call | flops 11000000512 | bytes 20000000 | tf_op jit(solution)/shard_map/decoder/pallas_call | solution.py:512
  147.6 1.7 %copy.11 = bf16[2,64,1024]{2,1,0:T(8,128)(2,1)} copy(bf16[2,64,1024]{2,1,0:T(8,128)(2,1)} %decoder.1) | data formatting | bytes 524288

commit v2 on v1

v2 whole, which is shorter than its diff:
```python
import math

import jax
import jax.numpy as jnp
import numpy as np
from jax import lax
from jax.experimental import pallas as pl
from jax.experimental.pallas import tpu as pltpu
from jax.sharding import PartitionSpec as P

MESH = pl.DeviceIdType.MESH
BF = jnp.bfloat16
F32 = jnp.float32
NX, NY, NZ = 4, 4, 8
SCALE = 1.0 / math.sqrt(128)

RING = [
    (0, 2), (0, 3), (0, 4), (1, 1), (0, 5), (1, 2), (1, 3), (1, 4), (2, 1), (1, 5), (2, 2), (2, 3), (3, 1), (2, 4), (2, 5),
    (3, 2), (3, 3), (3, 4), (4, 1), (3, 5), (4, 2), (4, 3), (4, 4), (4, 5),
]
PIECES = (((0, 32), (32, 32), (64, 32), (96, 16)), ((0, 32), (32, 32), (64, 32), (96, 32)), ((0, 512), (512, 512)))
WHOLE = (112, 128, 1024)

PROJECT, ATTEND, UPDATE, RENEW = range(4)
ORDER = "Q000 Q001 T000 T001 Q010 O000 O001 Q011 R000 T010 R001 T011 Q100 O010 Q101 O011".split()
ORDER += "R010 T100 R011 Q110 O100 Q111 T101 T110 T111 O101 O110 O111 R100 R101 R110 R111".split()
CODES = [8 * "QTOR".index(e[0]) + int(e[1:], 2) for e in ORDER]
WORDS = [sum(code << (5 * n) for n, code in enumerate(CODES[i : i + 4])) for i in range(0, 32, 4)]


def remote(src, dst, send_sem, recv_sem, device):
    return pltpu.make_async_remote_copy(
        src_ref=src,
        dst_ref=dst,
        send_sem=send_sem,
        recv_sem=recv_sem,
        device_id=device,
        device_id_type=MESH,
    )


def kernel(
    text, patches, tokens, conn, wq, wkv, wo, cosine, sine, out,
    CN, WQ, WO, PNS, PN, TS, T0, IS, IR, H, QS, QR, KS, VS, AR, OS, OR, FS, FR,
    own_s, own_r, z_s, z_r, f_s, f_r, p_s, p_r, t_s, t_r, i_s, i_r,
    h_s, h_r, q_s, q_r, a_s, a_r, o_s, o_r, e_s, e_r,
):
    c = lax.axis_index("pipe")
    d = lax.axis_index("dp")
    y = lax.axis_index("tensor")
    z = lax.div(d, NX)
    x = lax.rem(d, NX)

    def at(core, zz, xx, yy):
        return (core, zz * NX + xx, yy)

    def xk(k):
        return lax.rem(x + k, NX)

    def yk(k):
        return lax.rem(y + k, NY)

    def zk(k):
        return lax.rem(z + k + NZ, NZ)

    barrier = pltpu.get_barrier_semaphore()
    greeted = [at(1 - c, z, xk(k), y) for k in range(4)]
    greeted += [at(c, z, xk(k), y) for k in range(1, 4)]
    greeted += [at(c, z, x, yk(k)) for k in range(1, 4)]
    greeted += [at(c, zk(1), x, y), at(c, zk(-1), x, y)]
    for device in greeted:
        pl.semaphore_signal(barrier, inc=1, device_id=device, device_id_type=MESH)
    pl.semaphore_wait(barrier, len(greeted))

    zrow = pl.multiple_of(z * 128, 128)
    WQ[c, pl.ds(zrow, 128), pl.ds(0, 1024)] = wq[0]
    WQ[c, pl.ds(zrow, 128), pl.ds(1024, 256)] = wkv[0, 0]
    WQ[c, pl.ds(zrow, 128), pl.ds(1280, 256)] = wkv[0, 1]
    WO[c, :, pl.ds(zrow, 128)] = wo[0]
    CN[z, pl.ds(0, 96)] = conn[pl.ds(0, 96)]
    CN[z, pl.ds(96, 16)] = jnp.zeros((16, 1024), BF)
    CN[z, pl.ds(96, 4)] = conn[pl.ds(96, 4)]

    def kind(item):
        return 0 if item == 0 else 2 - item % 2

    def rows_of(item, zz, start, size):
        s = (item - 1) // 2
        if item == 0:
            return CN.at[zz, pl.ds(start, size)]
        if item % 2 == 1:
            return WQ.at[s, pl.ds(pl.multiple_of(zz * 128 + start, 32), size)]
        return WO.at[s, pl.ds(start, size), pl.ds(pl.multiple_of(zz * 128, 128), 128)]

    def block(item, zz):
        return rows_of(item, zz, 0, WHOLE[kind(item)])

    def own_copy(s, n):
        ref = block(1 + 2 * s + n, z)
        return remote(ref, ref, own_s.at[n], own_r.at[n], at(1 - s, z, x, y))

    def piece_ways(item, step):
        count = len(PIECES[kind(item)])
        return [(p, w) for p in range(count) for w in range(2) if step < 4 or p // (count // 2) == w]

    def piece_copy(item, step, piece, way, arriving):
        hops = step if arriving else step - 1
        zz = zk(-hops) if way == 0 else zk(hops)
        ref = rows_of(item, zz, *PIECES[kind(item)][piece])
        target = at(1, zk(1) if way == 0 else zk(-1), x, y)
        index = (item, step - 1, way, piece)
        return remote(ref, ref, z_s.at[index], z_r.at[index], target)

    def hand_over(item, index):
        step = index // 2 + 1
        zz = zk(-step) if index % 2 == 0 else zk(step)
        ref = block(item, zz)
        return remote(ref, ref, f_s.at[item, index], f_r.at[item, index], at(0, z, x, y))

    def patch_copy(k):
        return remote(PNS.at[xk(k)], PN.at[x, :, c], p_s.at[k], p_r.at[x, c], at(0, z, xk(k), y))

    def patch_arrival(source, core):
        ref = PN.at[source, :, core]
        return remote(ref, ref, p_s.at[0], p_r.at[source, core], at(0, z, x, y))

    def normed_patches():
        values = patches[...].reshape(64, 3200).astype(F32)
        centered = values - jnp.sum(values, axis=-1, keepdims=True) / 3200.0
        variance = jnp.sum(centered * centered, axis=-1, keepdims=True) / 3200.0
        normed = centered * lax.rsqrt(variance + 1e-06)
        row = lax.broadcasted_iota(jnp.int32, (64, 1), 0)
        limit = jnp.where(row < 32, tokens[0], tokens[1])
        normed = jnp.where(c * 32 + lax.rem(row, 32) < limit, normed, 0.0)
        lane = lax.broadcasted_iota(jnp.int32, (64, 128), 1)
        for j in range(32):
            zz, xx = divmod(j, NX)
            base = (100 * j) // 128 * 128
            offset = 100 * j - base
            width = 128 if offset + 100 <= 128 else 256
            window = normed[:, base : base + width]
            if offset:
                window = pltpu.roll(window, width - offset, 1)
            part = jnp.where(lane < 100, window[:, :128], 0.0)
            PNS[xx, :, :, zz * 128 : (zz + 1) * 128] = part.astype(BF).reshape(2, 32, 128)

    @pl.when(c == 1)
    def _():
        own = [own_copy(1, 0), own_copy(1, 1)]
        for copy in own:
            copy.start()
        for piece, way in piece_ways(0, 1):
            piece_copy(0, 1, piece, way, False).start()
        normed_patches()
        for k in range(4):
            patch_copy(k).start()
        for item, step in RING:
            onward = piece_ways(item, step) if step < 5 else []
            if step == 1:
                if item in (1, 2):
                    own_copy(0, item - 1).wait_recv()
                for piece, way in onward:
                    piece_copy(item, 1, piece, way, False).start()
            else:
                for piece, way in piece_ways(item, step - 1):
                    piece_copy(item, step - 1, piece, way, True).wait_recv()
                    if (piece, way) in onward:
                        piece_copy(item, step, piece, way, False).start()
                for index in (6,) if step == 5 else (2 * step - 4, 2 * step - 3):
                    hand_over(item, index).start()
        for copy in own:
            copy.wait_send()
        for k in range(4):
            patch_copy(k).wait_send()
        for item in range(5):
            for step in range(1, 5):
                for piece, way in piece_ways(item, step):
                    piece_copy(item, step, piece, way, False).wait_send()
            for index in range(7):
                hand_over(item, index).wait_send()

    def wait_item(item):
        for index in range(7):
            hand_over(item, index).wait_recv()

    def text_copy(half, k):
        target = at(0, z, xk(k), y)
        if half == 1:
            return remote(TS.at[xk(k), :, 1], H.at[0, :, 1, y, x], t_s.at[1, k], t_r.at[1, x], target)
        return remote(TS.at[xk(k), :, 0], T0.at[:, x], t_s.at[0, k], t_r.at[0, x], target)

    def text_arrival(half, k):
        ref = H.at[0, :, 1, y, xk(k)] if half == 1 else T0.at[:, xk(k)]
        return remote(ref, ref, t_s.at[half, k], t_r.at[half, xk(k)], at(1, z, x, y))

    def image_copy(b, k):
        return remote(IS.at[b, xk(k)], IR.at[b, x], i_s.at[b, k], i_r.at[b, x], at(0, z, xk(k), y))

    def image_arrival(b, k):
        ref = IR.at[b, xk(k)]
        return remote(ref, ref, i_s.at[b, k], i_r.at[b, xk(k)], at(1, z, x, y))

    def hidden_copy(s, b, h, k):
        ref = H.at[s, b, h, y]
        return remote(ref, ref, h_s.at[s, b, h, k], h_r.at[s, b, h, y], at(0, z, x, yk(k)))

    def hidden_arrival(s, b, h, k):
        ref = H.at[s, b, h, yk(k)]
        return remote(ref, ref, h_s.at[s, b, h, k], h_r.at[s, b, h, yk(k)], at(1, z, x, y))

    def qkv_copy(s, b, h, k):
        return remote(
            QS.at[s, b, h, xk(k)], QR.at[s, b, h, x], q_s.at[s, b, h, k], q_r.at[s, b, h, x], at(0, z, xk(k), y)
        )

    def qkv_arrival(s, b, h, k):
        ref = QR.at[s, b, h, xk(k)]
        return remote(ref, ref, q_s.at[s, b, h, k], q_r.at[s, b, h, xk(k)], at(1, z, x, y))

    def attended_copy(s, b, h, k):
        ref = AR.at[s, b, h, x]
        return remote(ref, ref, a_s.at[s, b, h, k], a_r.at[s, b, h, x], at(0, z, xk(k), y))

    def attended_arrival(s, b, h, k):
        ref = AR.at[s, b, h, xk(k)]
        return remote(ref, ref, a_s.at[s, b, h, k], a_r.at[s, b, h, xk(k)], at(1, z, x, y))

    def update_copy(s, b, h, k):
        return remote(
            OS.at[s, b, h, yk(k)], OR.at[s, b, h, y], o_s.at[s, b, h, k], o_r.at[s, b, h, y], at(0, z, x, yk(k))
        )

    def update_arrival(s, b, h, k):
        ref = OR.at[s, b, h, yk(k)]
        return remote(ref, ref, o_s.at[s, b, h, k], o_r.at[s, b, h, yk(k)], at(1, z, x, y))

    def final_copy(b, h, k):
        return remote(FS.at[b, h, xk(k)], FR.at[x, b], e_s.at[b, h, k], e_r.at[x, b], at(h, z, xk(k), y))

    def final_arrival(b, k):
        ref = FR.at[xk(k), b]
        return remote(ref, ref, e_s.at[b, 0, k], e_r.at[xk(k), b], at(1 - c, z, x, y))

    def send_text():
        position = lax.broadcasted_iota(jnp.int32, (128, 1), 0)
        for b in range(2):
            masked = jnp.where(position < tokens[b], jnp.zeros_like(text[b]), text[b])
            for xx in range(NX):
                for zz in range(2):
                    lanes = zz * 512 + xx * 128
                    TS[xx, b, :, :, zz * 128 : (zz + 1) * 128] = masked[:, lanes : lanes + 128].reshape(2, 64, 128)
        for b in range(2):
            H[0, b, 1, y, x] = TS[x, b, 1]
            T0[b, x] = TS[x, b, 0]
        for half in (1, 0):
            for k in range(1, 4):
                text_copy(half, k).start()

    def image_part():
        for core in range(2):
            for k in range(1 - core, 4):
                patch_arrival(xk(k), core).wait_recv()
        wait_item(0)
        for b in range(2):
            rows = PN[:, b].reshape(256, 1024)
            for zz in range(2):
                for pair in range(2):
                    lanes = zz * 512 + pair * 256
                    product = jnp.dot(
                        rows, CN[:, :, lanes : lanes + 256].reshape(1024, 256), preferred_element_type=F32
                    ).astype(BF)
                    for n in range(2):
                        part = product[:, n * 128 : (n + 1) * 128]
                        IS[b, 2 * pair + n, :, :, zz * 128 : (zz + 1) * 128] = part.reshape(4, 64, 128)
            for k in range(1, 4):
                image_copy(b, k).start()
        for k in range(1, 4):
            text_arrival(0, k).wait_recv()
        for b in range(2):
            for k in range(1, 4):
                image_arrival(b, k).wait_recv()
            total = IS[b, x].astype(F32)
            for k in range(1, 4):
                total = total + IR[b, xk(k)].astype(F32)
            H[0, b, 0, y] = (total.astype(BF).astype(F32) + T0[b].astype(F32)).astype(BF)
            for k in range(1, 4):
                hidden_copy(0, b, 0, k).start()

    def project(s, b, h):
        squares = jnp.zeros((256, 256), F32)
        for q in range(4):
            values = H[s, b, h, q].reshape(256, 256).astype(F32)
            squares = squares + values * values
        squares = jnp.sum(squares, axis=-1, keepdims=True)
        high = squares.astype(BF).astype(F32)
        lane = lax.broadcasted_iota(jnp.int32, (256, 128), 1)
        QS[s, b, h, :, :, 1536:1664] = (
            jnp.where(lane < 64, high, squares - high).astype(BF).reshape(4, 64, 128)
        )

        def tile(n, _):
            lanes = pl.ds(pl.multiple_of(n * 256, 256), 256)
            total = jnp.zeros((256, 256), F32)
            for q in range(4):
                total = total + jnp.dot(
                    H[s, b, h, q].reshape(256, 256),
                    WQ[s, pl.ds(q * 256, 256), lanes],
                    preferred_element_type=F32,
                )
            QS[s, b, h, :, :, lanes] = total.astype(BF).reshape(4, 64, 256)
            return 0

        lax.fori_loop(0, 6, tile, 0)
        for k in range(1, 4):
            qkv_copy(s, b, h, k).start()

    def attend(s, b, h):
        for k in range(1, 4):
            qkv_arrival(s, b, h, k).wait_recv()

        def summed(start):
            lanes = slice(start, start + 128)
            total = QS[s, b, h, x, :, lanes].astype(F32)
            for k in range(1, 4):
                total = total + QR[s, b, h, xk(k), :, lanes].astype(F32)
            return total

        squares = summed(1536)
        scale = lax.rsqrt((squares[:, 0:1] + squares[:, 64:65]) / 4096.0 + 1e-05)
        half = pl.ds(pl.multiple_of(h * 64, 64), 64)
        cos_rows = cosine[half]
        sin_rows = sine[half]

        def rotated(start):
            rows = summed(start) * scale
            return (rows * cos_rows + pltpu.roll(rows, 64, 1) * sin_rows).astype(BF)

        row = lax.rem(lax.broadcasted_iota(jnp.int32, (256, 128), 0), 64) + h * 64
        column = lax.broadcasted_iota(jnp.int32, (256, 128), 1)
        for g in range(2):
            KS[b, g, half] = rotated(1024 + g * 128)
            VS[b, g, half] = (summed(1280 + g * 128) * scale).astype(BF)
            stacked = jnp.concatenate([rotated((4 * g + j) * 128) for j in range(4)], axis=0)
            scores = lax.dot_general(
                stacked, KS[b, g], (((1,), (1,)), ((), ())), preferred_element_type=F32
            )
            scores = jnp.where(row >= column, scores * SCALE, -1e30)
            weights = jnp.exp(scores - jnp.max(scores, axis=-1, keepdims=True))
            norm = jnp.sum(weights, axis=-1, keepdims=True)
            mixed = jnp.dot(weights.astype(BF), VS[b, g], preferred_element_type=F32) / norm
            for j in range(4):
                lanes = (4 * g + j) * 128
                AR[s, b, h, x, :, lanes : lanes + 128] = mixed[j * 64 : (j + 1) * 64].astype(BF)
        for k in range(1, 4):
            attended_copy(s, b, h, k).start()

    def update(s, b, h):
        for k in range(1, 4):
            attended_arrival(s, b, h, k).wait_recv()

        def tile(n, _):
            yd = yk(n + 1)
            lanes = pl.ds(pl.multiple_of(yd * 256, 256), 256)
            product = jnp.dot(AR[s, b, h].reshape(256, 1024), WO[s, :, lanes], preferred_element_type=F32)
            OS[s, b, h, yd] = product.astype(BF).reshape(4, 64, 256)

            @pl.when(n < 3)
            def _():
                update_copy(s, b, h, n + 1).start()

            return 0

        lax.fori_loop(0, 4, tile, 0)

    def renew(s, b, h):
        for k in range(1, 4):
            update_arrival(s, b, h, k).wait_recv()
        total = OS[s, b, h, y].astype(F32)
        for k in range(1, 4):
            total = total + OR[s, b, h, yk(k)].astype(F32)
        fresh = (H[s, b, h, y].astype(F32) + total).astype(BF)

        @pl.when(s == 0)
        def _():
            H[1, b, h, y] = fresh
            for k in range(1, 4):
                hidden_copy(1, b, h, k).start()

        @pl.when(s == 1)
        def _():
            FS[b, h] = fresh
            for k in range(1, 4):
                final_copy(b, h, k).start()

            @pl.when(h == 0)
            def _():
                FR[x, b] = FS[b, 0, x]

            @pl.when(h == 1)
            def _():
                final_copy(b, h, 0).start()

    @pl.when(c == 0)
    def _():
        own_copy(0, 0).start()
        own_copy(0, 1).start()
        send_text()
        for zz in range(NZ):
            CN[zz, pl.ds(112, 16)] = jnp.zeros((16, 1024), BF)
        KS[...] = jnp.zeros_like(KS)
        VS[...] = jnp.zeros_like(VS)
        normed_patches()
        PN[x, :, 0] = PNS[x]
        for k in range(1, 4):
            patch_copy(k).start()
        for k in range(1, 4):
            text_arrival(1, k).wait_recv()
        for b in range(2):
            for k in range(1, 4):
                hidden_copy(0, b, 1, k).start()
        image_part()

        def stage(n, word):
            fresh = jnp.int32(WORDS[7])
            for m in range(7):
                fresh = jnp.where(lax.div(n, 4) == m, jnp.int32(WORDS[m]), fresh)
            word = jnp.where(lax.rem(n, 4) == 0, fresh, word)
            code = lax.rem(word, 32)
            what = lax.div(code, 8)
            s = lax.rem(lax.div(code, 4), 2)
            b = lax.rem(lax.div(code, 2), 2)
            h = lax.rem(code, 2)
            first = lax.rem(code, 4) == 0

            @pl.when(what == PROJECT)
            def _():
                @pl.when(first & (s == 0))
                def _():
                    wait_item(1)

                @pl.when(first & (s == 1))
                def _():
                    own_copy(1, 0).wait_recv()
                    wait_item(3)

                for k in range(1, 4):
                    hidden_arrival(s, b, h, k).wait_recv()
                project(s, b, h)

            @pl.when(what == ATTEND)
            def _():
                attend(s, b, h)

            @pl.when(what == UPDATE)
            def _():
                @pl.when(first & (s == 0))
                def _():
                    wait_item(2)

                @pl.when(first & (s == 1))
                def _():
                    own_copy(1, 1).wait_recv()
                    wait_item(4)

                update(s, b, h)

            @pl.when(what == RENEW)
            def _():
                renew(s, b, h)

            return lax.div(word, 32)

        lax.fori_loop(0, 32, stage, jnp.int32(0))

    for b in range(2):

        @pl.when(c == 1)
        def _():
            final_arrival(b, 0).wait_recv()

        for k in range(1, 4):
            final_arrival(b, k).wait_recv()
    for b in range(2):
        for xx in range(NX):
            for zz in range(2):
                lanes = zz * 512 + xx * 128
                out[b, :, lanes : lanes + 128] = FR[xx, b, :, zz * 128 : (zz + 1) * 128]

    @pl.when(c == 0)
    def _():
        own_copy(0, 0).wait_send()
        own_copy(0, 1).wait_send()
        for k in range(1, 4):
            patch_copy(k).wait_send()
            text_copy(0, k).wait_send()
            text_copy(1, k).wait_send()
            image_copy(0, k).wait_send()
            image_copy(1, k).wait_send()

        def drain(n, _):
            s, b = lax.div(n, 2), lax.rem(n, 2)
            for k in range(1, 4):
                for h in range(2):
                    hidden_copy(s, b, h, k).wait_send()
                    qkv_copy(s, b, h, k).wait_send()
                    attended_copy(s, b, h, k).wait_send()
                    update_copy(s, b, h, k).wait_send()
            return 0

        lax.fori_loop(0, 4, drain, 0)
        for b in range(2):
            for h in range(2):
                for k in range(1 - h, 4):
                    final_copy(b, h, k).wait_send()


def rotation_tables():
    frequencies = 500000.0 ** (-(np.arange(64, dtype=np.float32) * np.float32(2.0) / np.float32(128)))
    angles = np.arange(128, dtype=np.float32)[:, None] * frequencies.astype(np.float32)[None, :]
    cosine, sine = np.cos(angles), np.sin(angles)
    return (
        np.concatenate([cosine, cosine], axis=1).astype(np.float32),
        np.concatenate([-sine, sine], axis=1).astype(np.float32),
    )


def shards(text_embeds, patches, image_tokens, connector, w_query, w_keyval, w_out):
    cosine, sine = rotation_tables()
    vmem = pl.BlockSpec(memory_space=pltpu.VMEM)
    dma = pltpu.SemaphoreType.DMA
    return pl.pallas_call(
        kernel,
        out_shape=jax.ShapeDtypeStruct((2, 64, 1024), BF),
        in_specs=[vmem, vmem, pl.BlockSpec(memory_space=pltpu.SMEM)] + [vmem] * 6,
        out_specs=vmem,
        scratch_shapes=[
            pltpu.VMEM((8, 128, 1024), BF),
            pltpu.VMEM((2, 1024, 1536), BF),
            pltpu.VMEM((2, 1024, 1024), BF),
            pltpu.VMEM((4, 2, 32, 1024), BF),
            pltpu.VMEM((4, 2, 2, 32, 1024), BF),
            pltpu.VMEM((4, 2, 2, 64, 256), BF),
            pltpu.VMEM((2, 4, 64, 256), BF),
            pltpu.VMEM((2, 4, 4, 64, 256), BF),
            pltpu.VMEM((2, 4, 4, 64, 256), BF),
            pltpu.VMEM((2, 2, 2, 4, 4, 64, 256), BF),
            pltpu.VMEM((2, 2, 2, 4, 64, 1664), BF),
            pltpu.VMEM((2, 2, 2, 4, 64, 1664), BF),
            pltpu.VMEM((2, 2, 128, 128), BF),
            pltpu.VMEM((2, 2, 128, 128), BF),
            pltpu.VMEM((2, 2, 2, 4, 64, 1024), BF),
            pltpu.VMEM((2, 2, 2, 4, 4, 64, 256), BF),
            pltpu.VMEM((2, 2, 2, 4, 4, 64, 256), BF),
            pltpu.VMEM((2, 2, 4, 64, 256), BF),
            pltpu.VMEM((4, 2, 64, 256), BF),
            dma((2,)), dma((2,)),
            dma((5, 4, 2, 4)), dma((5, 4, 2, 4)),
            dma((5, 7)), dma((5, 7)),
            dma((4,)), dma((4, 2)),
            dma((2, 4)), dma((2, 4)),
            dma((2, 4)), dma((2, 4)),
            dma((2, 2, 2, 4)), dma((2, 2, 2, 4)),
            dma((2, 2, 2, 4)), dma((2, 2, 2, 4)),
            dma((2, 2, 2, 4)), dma((2, 2, 2, 4)),
            dma((2, 2, 2, 4)), dma((2, 2, 2, 4)),
            dma((2, 2, 4)), dma((4, 2)),
        ],
        compiler_params=pltpu.CompilerParams(
            collective_id=0, has_side_effects=True, vmem_limit_bytes=62 * 2**20
        ),
        cost_estimate=pl.CostEstimate(flops=11 * 10**9, bytes_accessed=20 * 10**6, transcendentals=10**6),
        name="decoder",
    )(text_embeds, patches, image_tokens, connector, w_query, w_keyval, w_out, cosine, sine)


def solution(mesh):
    placed = (
        P("dp", None, "tensor"),
        P("dp", "pipe", None),
        P("dp"),
        P("dp", "tensor"),
        P("pipe", "dp", "tensor"),
        P("pipe", None, "dp", "tensor"),
        P("pipe", "tensor", "dp"),
    )
    return jax.shard_map(
        shards, mesh=mesh, in_specs=placed, out_specs=P("dp", "pipe", "tensor"), check_vma=False
    )
```

time: 149 us -> 133 us (0.89)
  Pallas kernels: 146 us -> 131 us
  local copies, waits for them, and re-layouts: 3.31 us -> 1.67 us
    pallas_call x1, Pallas kernels: 146 us -> 131 us  [shards(): pl.pallas_call(kernel, out_shape=jax.ShapeDtypeStruct((2, 64, 1024), BF),...]
    pad x1 -> x0, local copies, waits for them, and re-layouts: 1.64 us -> none  [shards(): padded = jnp.pad(connector, ((0, 12), (0, 0)))]
where the time goes in v2:
time: 133 us
  Pallas kernels  131 us (98%)
  local copies, waits for them, and re-layouts  1.67 us (1%)
    pallas_call x1, Pallas kernels, shards(): pl.pallas_call(kernel, out_shape=jax.ShapeDtypeStruct((2, 64, 1024), BF),...  131 us

profile of v2, /device:TPU:1, one launch (start us, length us, event | category | flops | bytes accessed | tf_op | source)
XLA Modules:
  0.0 132.9 jit_solution(12754962811804868672)
XLA Ops:
  0.0 131.2 %decoder.1 = bf16[2,64,1024]{2,1,0:T(8,128)(2,1)} custom-call(bf16[2,128,1024]{2,1,0:T(8,128)(2,1)} %text.1, bf16[2,32,3200]{2,1,0:T(8,128)(2,1)} %patches.1, s32[2]{0:T(128)} %tokens.1, bf16[100,1024]{1,0:T(8,128)(2,1)} %conn.1, bf16[1,128,1024]{2,1,0:T(8,128)(2,1)} %wq.1, bf16[1,2,128,256]{3,2,1,0:T(8,128)(2,1)} %wkv.1, bf16[1,1024,128]{2,1,0:T(8,128)(2,1)} %wo.1, ...), custom_call_target="tpu_custom_call" | custom-call | flops 11000000512 | bytes 20000000 | tf_op jit(solution)/shard_map/decoder/pallas_call | solution.py:531
  131.2 1.7 %copy.11 = bf16[2,64,1024]{2,1,0:T(8,128)(2,1)} copy(bf16[2,64,1024]{2,1,0:T(8,128)(2,1)} %decoder.1) | data formatting | bytes 524288

commit v3 on v2

--- a/solution.py
+++ b/solution.py
@@ -15,16 +15,18 @@
 SCALE = 1.0 / math.sqrt(128)
 
 RING = [
-    (0, 2), (0, 3), (0, 4), (1, 1), (0, 5), (1, 2), (1, 3), (1, 4), (2, 1), (1, 5), (2, 2), (2, 3), (3, 1), (2, 4), (2, 5),
-    (3, 2), (3, 3), (3, 4), (4, 1), (3, 5), (4, 2), (4, 3), (4, 4), (4, 5),
+    (0, 2), (0, 3), (0, 4), (1, 2), (1, 3), (2, 1), (1, 4), (2, 2), (2, 3), (3, 1), (2, 4),
+    (3, 2), (3, 3), (4, 1), (3, 4), (4, 2), (4, 3), (4, 4),
 ]
 PIECES = (((0, 32), (32, 32), (64, 32), (96, 16)), ((0, 32), (32, 32), (64, 32), (96, 32)), ((0, 512), (512, 512)))
 WHOLE = (112, 128, 1024)
 
 PROJECT, ATTEND, UPDATE, RENEW = range(4)
-ORDER = "Q000 Q001 T000 T001 Q010 O000 O001 Q011 R000 T010 R001 T011 Q100 O010 Q101 O011".split()
-ORDER += "R010 T100 R011 Q110 O100 Q111 T101 T110 T111 O101 O110 O111 R100 R101 R110 R111".split()
-CODES = [8 * "QTOR".index(e[0]) + int(e[1:], 2) for e in ORDER]
+CODES = (
+    1, 0, 2, 8, 9, 3, 16, 10, 17, 24, 11, 25, 18, 4, 19, 5, 26, 27, 12, 6, 13, 20, 7, 21, 14, 15, 22, 23, 28, 29, 30, 31,
+)
+AWAITED = {8 * PROJECT: 1, 8 * PROJECT + 4: 3, 8 * UPDATE: 2, 8 * UPDATE + 4: 4}
+FIRST = {item: min(n for n, code in enumerate(CODES) if code // 4 == at // 4) for at, item in AWAITED.items()}
 WORDS = [sum(code << (5 * n) for n, code in enumerate(CODES[i : i + 4])) for i in range(0, 32, 4)]
 
 
@@ -67,7 +69,7 @@
     greeted = [at(1 - c, z, xk(k), y) for k in range(4)]
     greeted += [at(c, z, xk(k), y) for k in range(1, 4)]
     greeted += [at(c, z, x, yk(k)) for k in range(1, 4)]
-    greeted += [at(c, zk(1), x, y), at(c, zk(-1), x, y)]
+    greeted += [at(core, zk(way), x, y) for core in range(2) for way in (1, -1)]
     for device in greeted:
         pl.semaphore_signal(barrier, inc=1, device_id=device, device_id_type=MESH)
     pl.semaphore_wait(barrier, len(greeted))
@@ -107,22 +109,29 @@
         hops = step if arriving else step - 1
         zz = zk(-hops) if way == 0 else zk(hops)
         ref = rows_of(item, zz, *PIECES[kind(item)][piece])
-        target = at(1, zk(1) if way == 0 else zk(-1), x, y)
-        index = (item, step - 1, way, piece)
-        return remote(ref, ref, z_s.at[index], z_r.at[index], target)
+        target = at(1 if step < 4 else 0, zk(1) if way == 0 else zk(-1), x, y)
+        arrived = z_r.at[item % 3, step - 1, way, piece] if step < 4 else f_r.at[item]
+        return remote(ref, ref, z_s.at[item], arrived, target)
+
+    def blocks(item, count):
+        s = (item - 1) // 2
+        if item == 0:
+            return CN.at[pl.ds(0, count), pl.ds(0, 112)]
+        if item % 2 == 1:
+            return WQ.at[s, pl.ds(0, 128 * count)]
+        return WO.at[s, :, pl.ds(0, 128 * count)]
+
+    def waits(ref, semaphore):
+        return remote(ref, ref, semaphore, semaphore, at(1 - c, z, x, y))
 
     def hand_over(item, index):
         step = index // 2 + 1
         zz = zk(-step) if index % 2 == 0 else zk(step)
         ref = block(item, zz)
-        return remote(ref, ref, f_s.at[item, index], f_r.at[item, index], at(0, z, x, y))
+        return remote(ref, ref, f_s.at[item], f_r.at[item], at(0, z, x, y))
 
     def patch_copy(k):
-        return remote(PNS.at[xk(k)], PN.at[x, :, c], p_s.at[k], p_r.at[x, c], at(0, z, xk(k), y))
-
-    def patch_arrival(source, core):
-        ref = PN.at[source, :, core]
-        return remote(ref, ref, p_s.at[0], p_r.at[source, core], at(0, z, x, y))
+        return remote(PNS.at[xk(k)], PN.at[x, :, c], p_s.at[0], p_r.at[c], at(0, z, xk(k), y))
 
     def normed_patches():
         values = patches[...].reshape(64, 3200).astype(F32)
@@ -154,92 +163,79 @@
         normed_patches()
         for k in range(4):
             patch_copy(k).start()
+        own_copy(0, 0).wait_recv()
+        for way in range(2):
+            piece_copy(1, 1, 0, way, False).start()
         for item, step in RING:
-            onward = piece_ways(item, step) if step < 5 else []
             if step == 1:
-                if item in (1, 2):
-                    own_copy(0, item - 1).wait_recv()
-                for piece, way in onward:
+                if item == 2:
+                    own_copy(0, 1).wait_recv()
+                for piece, way in piece_ways(item, 1):
                     piece_copy(item, 1, piece, way, False).start()
             else:
+                onward = piece_ways(item, step)
                 for piece, way in piece_ways(item, step - 1):
                     piece_copy(item, step - 1, piece, way, True).wait_recv()
                     if (piece, way) in onward:
                         piece_copy(item, step, piece, way, False).start()
-                for index in (6,) if step == 5 else (2 * step - 4, 2 * step - 3):
+                if item == 0:
+                    for way in range(2):
+                        piece_copy(1, 1, step - 1, way, False).start()
+                for index in (2 * step - 4, 2 * step - 3):
                     hand_over(item, index).start()
         for copy in own:
             copy.wait_send()
-        for k in range(4):
-            patch_copy(k).wait_send()
+        waits(PNS, p_s.at[0]).wait_send()
         for item in range(5):
-            for step in range(1, 5):
-                for piece, way in piece_ways(item, step):
-                    piece_copy(item, step, piece, way, False).wait_send()
-            for index in range(7):
-                hand_over(item, index).wait_send()
+            waits(blocks(item, 7), z_s.at[item]).wait_send()
+            waits(blocks(item, 6), f_s.at[item]).wait_send()
 
     def wait_item(item):
-        for index in range(7):
-            hand_over(item, index).wait_recv()
+        waits(blocks(item, 7), f_r.at[item]).wait_recv()
 
     def text_copy(half, k):
         target = at(0, z, xk(k), y)
         if half == 1:
-            return remote(TS.at[xk(k), :, 1], H.at[0, :, 1, y, x], t_s.at[1, k], t_r.at[1, x], target)
-        return remote(TS.at[xk(k), :, 0], T0.at[:, x], t_s.at[0, k], t_r.at[0, x], target)
-
-    def text_arrival(half, k):
-        ref = H.at[0, :, 1, y, xk(k)] if half == 1 else T0.at[:, xk(k)]
-        return remote(ref, ref, t_s.at[half, k], t_r.at[half, xk(k)], at(1, z, x, y))
+            return remote(TS.at[xk(k), :, 1], H.at[0, :, 1, y, x], t_s.at[0], t_r.at[1], target)
+        return remote(TS.at[xk(k), :, 0], T0.at[:, x], t_s.at[0], t_r.at[0], target)
+
+    def text_arrival(half):
+        waits(H.at[0, :, 1, y, pl.ds(0, 3)] if half == 1 else T0.at[:, pl.ds(0, 3)], t_r.at[half]).wait_recv()
 
     def image_copy(b, k):
-        return remote(IS.at[b, xk(k)], IR.at[b, x], i_s.at[b, k], i_r.at[b, x], at(0, z, xk(k), y))
-
-    def image_arrival(b, k):
-        ref = IR.at[b, xk(k)]
-        return remote(ref, ref, i_s.at[b, k], i_r.at[b, xk(k)], at(1, z, x, y))
+        return remote(IS.at[b, xk(k)], IR.at[b, x], i_s.at[0], i_r.at[b], at(0, z, xk(k), y))
+
+    def image_arrival(b):
+        waits(IR.at[b, pl.ds(0, 3)], i_r.at[b]).wait_recv()
 
     def hidden_copy(s, b, h, k):
         ref = H.at[s, b, h, y]
-        return remote(ref, ref, h_s.at[s, b, h, k], h_r.at[s, b, h, y], at(0, z, x, yk(k)))
-
-    def hidden_arrival(s, b, h, k):
-        ref = H.at[s, b, h, yk(k)]
-        return remote(ref, ref, h_s.at[s, b, h, k], h_r.at[s, b, h, yk(k)], at(1, z, x, y))
+        return remote(ref, ref, h_s.at[0], h_r.at[b, h], at(0, z, x, yk(k)))
+
+    def hidden_arrival(s, b, h):
+        waits(H.at[s, b, h, pl.ds(0, 3)], h_r.at[b, h]).wait_recv()
 
     def qkv_copy(s, b, h, k):
-        return remote(
-            QS.at[s, b, h, xk(k)], QR.at[s, b, h, x], q_s.at[s, b, h, k], q_r.at[s, b, h, x], at(0, z, xk(k), y)
-        )
-
-    def qkv_arrival(s, b, h, k):
-        ref = QR.at[s, b, h, xk(k)]
-        return remote(ref, ref, q_s.at[s, b, h, k], q_r.at[s, b, h, xk(k)], at(1, z, x, y))
+        return remote(QS.at[s, b, h, xk(k)], QR.at[s, b, h, x], q_s.at[0], q_r.at[b, h], at(0, z, xk(k), y))
+
+    def qkv_arrival(s, b, h):
+        waits(QR.at[s, b, h, pl.ds(0, 3)], q_r.at[b, h]).wait_recv()
 
     def attended_copy(s, b, h, k):
         ref = AR.at[s, b, h, x]
-        return remote(ref, ref, a_s.at[s, b, h, k], a_r.at[s, b, h, x], at(0, z, xk(k), y))
-
-    def attended_arrival(s, b, h, k):
-        ref = AR.at[s, b, h, xk(k)]
-        return remote(ref, ref, a_s.at[s, b, h, k], a_r.at[s, b, h, xk(k)], at(1, z, x, y))
+        return remote(ref, ref, a_s.at[0], a_r.at[b, h], at(0, z, xk(k), y))
+
+    def attended_arrival(s, b, h):
+        waits(AR.at[s, b, h, pl.ds(0, 3)], a_r.at[b, h]).wait_recv()
 
     def update_copy(s, b, h, k):
-        return remote(
-            OS.at[s, b, h, yk(k)], OR.at[s, b, h, y], o_s.at[s, b, h, k], o_r.at[s, b, h, y], at(0, z, x, yk(k))
-        )
-
-    def update_arrival(s, b, h, k):
-        ref = OR.at[s, b, h, yk(k)]
-        return remote(ref, ref, o_s.at[s, b, h, k], o_r.at[s, b, h, yk(k)], at(1, z, x, y))
+        return remote(OS.at[s, b, h, yk(k)], OR.at[s, b, h, y], o_s.at[0], o_r.at[b, h], at(0, z, x, yk(k)))
+
+    def update_arrival(s, b, h):
+        waits(OR.at[s, b, h, pl.ds(0, 3)], o_r.at[b, h]).wait_recv()
 
     def final_copy(b, h, k):
-        return remote(FS.at[b, h, xk(k)], FR.at[x, b], e_s.at[b, h, k], e_r.at[x, b], at(h, z, xk(k), y))
-
-    def final_arrival(b, k):
-        ref = FR.at[xk(k), b]
-        return remote(ref, ref, e_s.at[b, 0, k], e_r.at[xk(k), b], at(1 - c, z, x, y))
+        return remote(FS.at[b, h, xk(k)], FR.at[x, b], e_s.at[h], e_r.at[b], at(h, z, xk(k), y))
 
     def send_text():
         position = lax.broadcasted_iota(jnp.int32, (128, 1), 0)
@@ -257,9 +253,8 @@
                 text_copy(half, k).start()
 
     def image_part():
-        for core in range(2):
-            for k in range(1 - core, 4):
-                patch_arrival(xk(k), core).wait_recv()
+        waits(PN.at[pl.ds(0, 3), :, 0], p_r.at[0]).wait_recv()
+        waits(PN.at[:, :, 1], p_r.at[1]).wait_recv()
         wait_item(0)
         for b in range(2):
             rows = PN[:, b].reshape(256, 1024)
@@ -274,11 +269,9 @@
                         IS[b, 2 * pair + n, :, :, zz * 128 : (zz + 1) * 128] = part.reshape(4, 64, 128)
             for k in range(1, 4):
                 image_copy(b, k).start()
-        for k in range(1, 4):
-            text_arrival(0, k).wait_recv()
+        text_arrival(0)
         for b in range(2):
-            for k in range(1, 4):
-                image_arrival(b, k).wait_recv()
+            image_arrival(b)
             total = IS[b, x].astype(F32)
             for k in range(1, 4):
                 total = total + IR[b, xk(k)].astype(F32)
@@ -315,8 +308,7 @@
             qkv_copy(s, b, h, k).start()
 
     def attend(s, b, h):
-        for k in range(1, 4):
-            qkv_arrival(s, b, h, k).wait_recv()
+        qkv_arrival(s, b, h)
 
         def summed(start):
             lanes = slice(start, start + 128)
@@ -355,8 +347,7 @@
             attended_copy(s, b, h, k).start()
 
     def update(s, b, h):
-        for k in range(1, 4):
-            attended_arrival(s, b, h, k).wait_recv()
+        attended_arrival(s, b, h)
 
         def tile(n, _):
             yd = yk(n + 1)
@@ -373,8 +364,7 @@
         lax.fori_loop(0, 4, tile, 0)
 
     def renew(s, b, h):
-        for k in range(1, 4):
-            update_arrival(s, b, h, k).wait_recv()
+        update_arrival(s, b, h)
         total = OS[s, b, h, y].astype(F32)
         for k in range(1, 4):
             total = total + OR[s, b, h, yk(k)].astype(F32)
@@ -413,8 +403,7 @@
         PN[x, :, 0] = PNS[x]
         for k in range(1, 4):
             patch_copy(k).start()
-        for k in range(1, 4):
-            text_arrival(1, k).wait_recv()
+        text_arrival(1)
         for b in range(2):
             for k in range(1, 4):
                 hidden_copy(0, b, 1, k).start()
@@ -430,21 +419,18 @@
             s = lax.rem(lax.div(code, 4), 2)
             b = lax.rem(lax.div(code, 2), 2)
             h = lax.rem(code, 2)
-            first = lax.rem(code, 4) == 0
+
+            for item in range(1, 5):
+
+                @pl.when(n == FIRST[item])
+                def _():
+                    if item > 2:
+                        own_copy(1, item - 3).wait_recv()
+                    wait_item(item)
 
             @pl.when(what == PROJECT)
             def _():
-                @pl.when(first & (s == 0))
-                def _():
-                    wait_item(1)
-
-                @pl.when(first & (s == 1))
-                def _():
-                    own_copy(1, 0).wait_recv()
-                    wait_item(3)
-
-                for k in range(1, 4):
-                    hidden_arrival(s, b, h, k).wait_recv()
+                hidden_arrival(s, b, h)
                 project(s, b, h)
 
             @pl.when(what == ATTEND)
@@ -453,15 +439,6 @@
 
             @pl.when(what == UPDATE)
             def _():
-                @pl.when(first & (s == 0))
-                def _():
-                    wait_item(2)
-
-                @pl.when(first & (s == 1))
-                def _():
-                    own_copy(1, 1).wait_recv()
-                    wait_item(4)
-
                 update(s, b, h)
 
             @pl.when(what == RENEW)
@@ -473,13 +450,15 @@
         lax.fori_loop(0, 32, stage, jnp.int32(0))
 
     for b in range(2):
+
+        @pl.when(c == 0)
+        def _():
+            waits(FR.at[pl.ds(0, 3), b], e_r.at[b]).wait_recv()
 
         @pl.when(c == 1)
         def _():
-            final_arrival(b, 0).wait_recv()
-
-        for k in range(1, 4):
-            final_arrival(b, k).wait_recv()
+            waits(FR.at[:, b], e_r.at[b]).wait_recv()
+
     for b in range(2):
         for xx in range(NX):
             for zz in range(2):
@@ -490,28 +469,13 @@
     def _():
         own_copy(0, 0).wait_send()
         own_copy(0, 1).wait_send()
-        for k in range(1, 4):
-            patch_copy(k).wait_send()
-            text_copy(0, k).wait_send()
-            text_copy(1, k).wait_send()
-            image_copy(0, k).wait_send()
-            image_copy(1, k).wait_send()
-
-        def drain(n, _):
-            s, b = lax.div(n, 2), lax.rem(n, 2)
-            for k in range(1, 4):
-                for h in range(2):
-                    hidden_copy(s, b, h, k).wait_send()
-                    qkv_copy(s, b, h, k).wait_send()
-                    attended_copy(s, b, h, k).wait_send()
-                    update_copy(s, b, h, k).wait_send()
-            return 0
-
-        lax.fori_loop(0, 4, drain, 0)
-        for b in range(2):
-            for h in range(2):
-                for k in range(1 - h, 4):
-                    final_copy(b, h, k).wait_send()
+        waits(PNS.at[pl.ds(0, 3)], p_s.at[0]).wait_send()
+        waits(TS.at[pl.ds(0, 3)], t_s.at[0]).wait_send()
+        waits(IS.at[:, pl.ds(0, 3)], i_s.at[0]).wait_send()
+        for sent, semaphore in ((H, h_s), (QS, q_s), (AR, a_s), (OS, o_s)):
+            waits(sent.at[:, :, :, pl.ds(0, 3)], semaphore.at[0]).wait_send()
+        waits(FS.at[:, 0, pl.ds(0, 3)], e_s.at[0]).wait_send()
+        waits(FS.at[:, 1], e_s.at[1]).wait_send()
 
 
 def rotation_tables():
@@ -554,16 +518,16 @@
             pltpu.VMEM((2, 2, 4, 64, 256), BF),
             pltpu.VMEM((4, 2, 64, 256), BF),
             dma((2,)), dma((2,)),
-            dma((5, 4, 2, 4)), dma((5, 4, 2, 4)),
-            dma((5, 7)), dma((5, 7)),
-            dma((4,)), dma((4, 2)),
-            dma((2, 4)), dma((2, 4)),
-            dma((2, 4)), dma((2, 4)),
-            dma((2, 2, 2, 4)), dma((2, 2, 2, 4)),
-            dma((2, 2, 2, 4)), dma((2, 2, 2, 4)),
-            dma((2, 2, 2, 4)), dma((2, 2, 2, 4)),
-            dma((2, 2, 2, 4)), dma((2, 2, 2, 4)),
-            dma((2, 2, 4)), dma((4, 2)),
+            dma((5,)), dma((3, 3, 2, 4)),
+            dma((5,)), dma((5,)),
+            dma((1,)), dma((2,)),
+            dma((1,)), dma((2,)),
+            dma((1,)), dma((2,)),
+            dma((1,)), dma((2, 2)),
+            dma((1,)), dma((2, 2)),
+            dma((1,)), dma((2, 2)),
+            dma((1,)), dma((2, 2)),
+            dma((2,)), dma((2,)),
         ],
         compiler_params=pltpu.CompilerParams(
             collective_id=0, has_side_effects=True, vmem_limit_bytes=62 * 2**20

time: 133 us -> 125 us (0.940)
  Pallas kernels: 131 us -> 124 us
    pallas_call x1, Pallas kernels: 131 us -> 124 us  [shards(): pl.pallas_call(kernel, out_shape=jax.ShapeDtypeStruct((2, 64, 1024), BF),...]
where the time goes in v3:
time: 125 us
  Pallas kernels  124 us (99%)
  local copies, waits for them, and re-layouts  1.67 us (1%)
    pallas_call x1, Pallas kernels, shards(): pl.pallas_call(kernel, out_shape=jax.ShapeDtypeStruct((2, 64, 1024), BF),...  124 us

profile of v3, /device:TPU:1, one launch (start us, length us, event | category | flops | bytes accessed | tf_op | source)
XLA Modules:
  0.0 125.3 jit_solution(14692215098104493913)
XLA Ops:
  0.0 123.6 %decoder.1 = bf16[2,64,1024]{2,1,0:T(8,128)(2,1)} custom-call(bf16[2,128,1024]{2,1,0:T(8,128)(2,1)} %text.1, bf16[2,32,3200]{2,1,0:T(8,128)(2,1)} %patches.1, s32[2]{0:T(128)} %tokens.1, bf16[100,1024]{1,0:T(8,128)(2,1)} %conn.1, bf16[1,128,1024]{2,1,0:T(8,128)(2,1)} %wq.1, bf16[1,2,128,256]{3,2,1,0:T(8,128)(2,1)} %wkv.1, bf16[1,1024,128]{2,1,0:T(8,128)(2,1)} %wo.1, ...), custom_call_target="tpu_custom_call" | custom-call | flops 11000000512 | bytes 20000000 | tf_op jit(solution)/shard_map/decoder/pallas_call | solution.py:495
  123.6 1.7 %copy.11 = bf16[2,64,1024]{2,1,0:T(8,128)(2,1)} copy(bf16[2,64,1024]{2,1,0:T(8,128)(2,1)} %decoder.1) | data formatting | bytes 524288

commit v4 on v3

--- a/solution.py
+++ b/solution.py
@@ -15,7 +15,7 @@
 SCALE = 1.0 / math.sqrt(128)
 
 RING = [
-    (0, 2), (0, 3), (0, 4), (1, 2), (1, 3), (2, 1), (1, 4), (2, 2), (2, 3), (3, 1), (2, 4),
+    (0, 2), (0, 3), (0, 4), (1, 2), (1, 3), (1, 4), (2, 1), (2, 2), (2, 3), (3, 1), (2, 4),
     (3, 2), (3, 3), (4, 1), (3, 4), (4, 2), (4, 3), (4, 4),
 ]
 PIECES = (((0, 32), (32, 32), (64, 32), (96, 16)), ((0, 32), (32, 32), (64, 32), (96, 32)), ((0, 512), (512, 512)))
@@ -42,9 +42,10 @@
 
 
 def kernel(
-    text, patches, tokens, conn, wq, wkv, wo, cosine, sine, out,
+    text_in, patches_in, tokens_in, conn_in, wq, wkv, wo, cosine_in, sine_in, out,
+    text, patches, tokens, conn, cosine, sine,
     CN, WQ, WO, PNS, PN, TS, T0, IS, IR, H, QS, QR, KS, VS, AR, OS, OR, FS, FR,
-    own_s, own_r, z_s, z_r, f_s, f_r, p_s, p_r, t_s, t_r, i_s, i_r,
+    l_s, own_s, own_r, z_s, z_r, f_s, f_r, p_s, p_r, t_s, t_r, i_s, i_r,
     h_s, h_r, q_s, q_r, a_s, a_r, o_s, o_r, e_s, e_r,
 ):
     c = lax.axis_index("pipe")
@@ -64,6 +65,23 @@
 
     def zk(k):
         return lax.rem(z + k + NZ, NZ)
+
+    zrow = pl.multiple_of(z * 128, 128)
+    local = [
+        (conn_in, conn),
+        (wq.at[0], WQ.at[c, pl.ds(zrow, 128), pl.ds(0, 1024)]),
+        (wkv.at[0, 0], WQ.at[c, pl.ds(zrow, 128), pl.ds(1024, 256)]),
+        (wkv.at[0, 1], WQ.at[c, pl.ds(zrow, 128), pl.ds(1280, 256)]),
+        (patches_in, patches),
+        (tokens_in, tokens),
+        (text_in, text),
+        (wo.at[0], WO.at[c, :, pl.ds(zrow, 128)]),
+        (cosine_in, cosine),
+        (sine_in, sine),
+    ]
+    loads = [pltpu.make_async_copy(a, b, l_s.at[n]) for n, (a, b) in enumerate(local)]
+    for load in loads:
+        load.start()
 
     barrier = pltpu.get_barrier_semaphore()
     greeted = [at(1 - c, z, xk(k), y) for k in range(4)]
@@ -74,11 +92,7 @@
         pl.semaphore_signal(barrier, inc=1, device_id=device, device_id_type=MESH)
     pl.semaphore_wait(barrier, len(greeted))
 
-    zrow = pl.multiple_of(z * 128, 128)
-    WQ[c, pl.ds(zrow, 128), pl.ds(0, 1024)] = wq[0]
-    WQ[c, pl.ds(zrow, 128), pl.ds(1024, 256)] = wkv[0, 0]
-    WQ[c, pl.ds(zrow, 128), pl.ds(1280, 256)] = wkv[0, 1]
-    WO[c, :, pl.ds(zrow, 128)] = wo[0]
+    loads[0].wait()
     CN[z, pl.ds(0, 96)] = conn[pl.ds(0, 96)]
     CN[z, pl.ds(96, 16)] = jnp.zeros((16, 1024), BF)
     CN[z, pl.ds(96, 4)] = conn[pl.ds(96, 4)]
@@ -155,11 +169,13 @@
 
     @pl.when(c == 1)
     def _():
+        for piece, way in piece_ways(0, 1):
+            piece_copy(0, 1, piece, way, False).start()
+        for load in loads[1:]:
+            load.wait()
         own = [own_copy(1, 0), own_copy(1, 1)]
         for copy in own:
             copy.start()
-        for piece, way in piece_ways(0, 1):
-            piece_copy(0, 1, piece, way, False).start()
         normed_patches()
         for k in range(4):
             patch_copy(k).start()
@@ -215,8 +231,11 @@
     def hidden_arrival(s, b, h):
         waits(H.at[s, b, h, pl.ds(0, 3)], h_r.at[b, h]).wait_recv()
 
-    def qkv_copy(s, b, h, k):
-        return remote(QS.at[s, b, h, xk(k)], QR.at[s, b, h, x], q_s.at[0], q_r.at[b, h], at(0, z, xk(k), y))
+    def qkv_copy(s, b, h, k, part):
+        rows = pl.ds(0, 384) if part == 0 else pl.ds(384, 400)
+        return remote(
+            QS.at[s, b, h, xk(k), rows], QR.at[s, b, h, x, rows], q_s.at[0], q_r.at[b, h], at(0, z, xk(k), y)
+        )
 
     def qkv_arrival(s, b, h):
         waits(QR.at[s, b, h, pl.ds(0, 3)], q_r.at[b, h]).wait_recv()
@@ -286,10 +305,11 @@
             squares = squares + values * values
         squares = jnp.sum(squares, axis=-1, keepdims=True)
         high = squares.astype(BF).astype(F32)
+        row = lax.rem(lax.broadcasted_iota(jnp.int32, (256, 128), 0), 64)
         lane = lax.broadcasted_iota(jnp.int32, (256, 128), 1)
-        QS[s, b, h, :, :, 1536:1664] = (
-            jnp.where(lane < 64, high, squares - high).astype(BF).reshape(4, 64, 128)
-        )
+        spread = jnp.where(lane == row, high, jnp.where(lane == row + 64, squares - high, 0.0))
+        spread = jnp.sum(spread.reshape(4, 64, 128), axis=1, keepdims=True)
+        QS[s, b, h, :, 768:784, :] = jnp.broadcast_to(spread, (4, 16, 128)).astype(BF)
 
         def tile(n, _):
             lanes = pl.ds(pl.multiple_of(n * 256, 256), 256)
@@ -300,25 +320,36 @@
                     WQ[s, pl.ds(q * 256, 256), lanes],
                     preferred_element_type=F32,
                 )
-            QS[s, b, h, :, :, lanes] = total.astype(BF).reshape(4, 64, 256)
+            for i in range(2):
+                rows = pl.ds(pl.multiple_of((2 * n + i) * 64, 64), 64)
+                QS[s, b, h, :, rows, :] = total[:, i * 128 : (i + 1) * 128].astype(BF).reshape(4, 64, 128)
+
+            @pl.when(n == 2)
+            def _():
+                for k in range(1, 4):
+                    qkv_copy(s, b, h, k, 0).start()
+
             return 0
 
         lax.fori_loop(0, 6, tile, 0)
         for k in range(1, 4):
-            qkv_copy(s, b, h, k).start()
+            qkv_copy(s, b, h, k, 1).start()
 
     def attend(s, b, h):
         qkv_arrival(s, b, h)
 
-        def summed(start):
-            lanes = slice(start, start + 128)
-            total = QS[s, b, h, x, :, lanes].astype(F32)
-            for k in range(1, 4):
-                total = total + QR[s, b, h, xk(k), :, lanes].astype(F32)
+        def summed(start, size=64):
+            rows = slice(start, start + size)
+            total = QS[s, b, h, x, rows].astype(F32)
+            for k in range(1, 4):
+                total = total + QR[s, b, h, xk(k), rows].astype(F32)
             return total
 
-        squares = summed(1536)
-        scale = lax.rsqrt((squares[:, 0:1] + squares[:, 64:65]) / 4096.0 + 1e-05)
+        row = lax.broadcasted_iota(jnp.int32, (64, 128), 0)
+        lane = lax.broadcasted_iota(jnp.int32, (64, 128), 1)
+        spread = jnp.where(lax.rem(lane, 64) == row, summed(768, 16)[0:1], 0.0)
+        squares = jnp.sum(spread, axis=-1, keepdims=True)
+        scale = lax.rsqrt(squares / 4096.0 + 1e-05)
         half = pl.ds(pl.multiple_of(h * 64, 64), 64)
         cos_rows = cosine[half]
         sin_rows = sine[half]
@@ -330,9 +361,9 @@
         row = lax.rem(lax.broadcasted_iota(jnp.int32, (256, 128), 0), 64) + h * 64
         column = lax.broadcasted_iota(jnp.int32, (256, 128), 1)
         for g in range(2):
-            KS[b, g, half] = rotated(1024 + g * 128)
-            VS[b, g, half] = (summed(1280 + g * 128) * scale).astype(BF)
-            stacked = jnp.concatenate([rotated((4 * g + j) * 128) for j in range(4)], axis=0)
+            KS[b, g, half] = rotated((8 + g) * 64)
+            VS[b, g, half] = (summed((10 + g) * 64) * scale).astype(BF)
+            stacked = jnp.concatenate([rotated((4 * g + j) * 64) for j in range(4)], axis=0)
             scores = lax.dot_general(
                 stacked, KS[b, g], (((1,), (1,)), ((), ())), preferred_element_type=F32
             )
@@ -392,7 +423,11 @@
 
     @pl.when(c == 0)
     def _():
+        for load in loads[1:4]:
+            load.wait()
         own_copy(0, 0).start()
+        for load in loads[4:]:
+            load.wait()
         own_copy(0, 1).start()
         send_text()
         for zz in range(NZ):
@@ -495,9 +530,15 @@
     return pl.pallas_call(
         kernel,
         out_shape=jax.ShapeDtypeStruct((2, 64, 1024), BF),
-        in_specs=[vmem, vmem, pl.BlockSpec(memory_space=pltpu.SMEM)] + [vmem] * 6,
+        in_specs=[pl.BlockSpec(memory_space=pl.ANY)] * 9,
         out_specs=vmem,
         scratch_shapes=[
+            pltpu.VMEM((2, 128, 1024), BF),
+            pltpu.VMEM((2, 32, 3200), BF),
+            pltpu.SMEM((2,), jnp.int32),
+            pltpu.VMEM((100, 1024), BF),
+            pltpu.VMEM((128, 128), F32),
+            pltpu.VMEM((128, 128), F32),
             pltpu.VMEM((8, 128, 1024), BF),
             pltpu.VMEM((2, 1024, 1536), BF),
             pltpu.VMEM((2, 1024, 1024), BF),
@@ -508,8 +549,8 @@
             pltpu.VMEM((2, 4, 4, 64, 256), BF),
             pltpu.VMEM((2, 4, 4, 64, 256), BF),
             pltpu.VMEM((2, 2, 2, 4, 4, 64, 256), BF),
-            pltpu.VMEM((2, 2, 2, 4, 64, 1664), BF),
-            pltpu.VMEM((2, 2, 2, 4, 64, 1664), BF),
+            pltpu.VMEM((2, 2, 2, 4, 784, 128), BF),
+            pltpu.VMEM((2, 2, 2, 4, 784, 128), BF),
             pltpu.VMEM((2, 2, 128, 128), BF),
             pltpu.VMEM((2, 2, 128, 128), BF),
             pltpu.VMEM((2, 2, 2, 4, 64, 1024), BF),
@@ -517,6 +558,7 @@
             pltpu.VMEM((2, 2, 2, 4, 4, 64, 256), BF),
             pltpu.VMEM((2, 2, 4, 64, 256), BF),
             pltpu.VMEM((4, 2, 64, 256), BF),
+            dma((10,)),
             dma((2,)), dma((2,)),
             dma((5,)), dma((3, 3, 2, 4)),
             dma((5,)), dma((5,)),

time: 125 us -> 119 us (0.952)
  Pallas kernels: 124 us -> 117 us
    pallas_call x1, Pallas kernels: 124 us -> 117 us  [shards(): pl.pallas_call(kernel, out_shape=jax.ShapeDtypeStruct((2, 64, 1024), BF),...]
where the time goes in v4:
time: 119 us; the launch traced here: 118 us
  Pallas kernels  117 us (98%)
  local copies, waits for them, and re-layouts  1.67 us (1%)
    pallas_call x1, Pallas kernels, shards(): pl.pallas_call(kernel, out_shape=jax.ShapeDtypeStruct((2, 64, 1024), BF),...  117 us

profile of v4, /device:TPU:1, one launch (start us, length us, event | category | flops | bytes accessed | tf_op | source)
XLA Modules:
  0.0 118.4 jit_solution(13012891742195392049)
XLA Ops:
  0.0 116.7 %decoder.1 = bf16[2,64,1024]{2,1,0:T(8,128)(2,1)} custom-call(bf16[2,128,1024]{2,1,0:T(8,128)(2,1)} %text_in.1, bf16[2,32,3200]{2,1,0:T(8,128)(2,1)} %patches_in.1, s32[2]{0:T(128)} %tokens_in.1, bf16[100,1024]{1,0:T(8,128)(2,1)} %conn_in.1, bf16[1,128,1024]{2,1,0:T(8,128)(2,1)} %wq.1, bf16[1,2,128,256]{3,2,1,0:T(8,128)(2,1)} %wkv.1, ...), custom_call_target="tpu_custom_call" | custom-call | flops 11000000512 | bytes 20000000 | tf_op jit(solution)/shard_map/decoder/pallas_call | solution.py:530
  116.7 1.7 %copy.11 = bf16[2,64,1024]{2,1,0:T(8,128)(2,1)} copy(bf16[2,64,1024]{2,1,0:T(8,128)(2,1)} %decoder.1) | data formatting | bytes 524288

commit v5 on v4

--- a/solution.py
+++ b/solution.py
@@ -13,6 +13,7 @@
 F32 = jnp.float32
 NX, NY, NZ = 4, 4, 8
 SCALE = 1.0 / math.sqrt(128)
+FAR_FIRST = (2, 1, 3)
 
 RING = [
     (0, 2), (0, 3), (0, 4), (1, 2), (1, 3), (1, 4), (2, 1), (2, 2), (2, 3), (3, 1), (2, 4),
@@ -84,13 +85,25 @@
         load.start()
 
     barrier = pltpu.get_barrier_semaphore()
-    greeted = [at(1 - c, z, xk(k), y) for k in range(4)]
-    greeted += [at(c, z, xk(k), y) for k in range(1, 4)]
-    greeted += [at(c, z, x, yk(k)) for k in range(1, 4)]
-    greeted += [at(core, zk(way), x, y) for core in range(2) for way in (1, -1)]
-    for device in greeted:
-        pl.semaphore_signal(barrier, inc=1, device_id=device, device_id_type=MESH)
-    pl.semaphore_wait(barrier, len(greeted))
+    both = [at(1 - c, z, xk(k), y) for k in range(4)] + [at(1 - c, zk(way), x, y) for way in (1, -1)]
+    plane = [at(0, z, xk(k), y) for k in range(1, 4)] + [at(0, z, x, yk(k)) for k in range(1, 4)]
+    line = [at(1, zk(way), x, y) for way in (1, -1)]
+
+    def greet(devices):
+        for device in devices:
+            pl.semaphore_signal(barrier, inc=1, device_id=device, device_id_type=MESH)
+
+    greet(both)
+
+    @pl.when(c == 0)
+    def _():
+        greet(plane)
+        pl.semaphore_wait(barrier, len(both) + len(plane))
+
+    @pl.when(c == 1)
+    def _():
+        greet(line)
+        pl.semaphore_wait(barrier, len(both) + len(line))
 
     loads[0].wait()
     CN[z, pl.ds(0, 96)] = conn[pl.ds(0, 96)]
@@ -240,8 +253,8 @@
     def qkv_arrival(s, b, h):
         waits(QR.at[s, b, h, pl.ds(0, 3)], q_r.at[b, h]).wait_recv()
 
-    def attended_copy(s, b, h, k):
-        ref = AR.at[s, b, h, x]
+    def attended_copy(s, b, h, k, g):
+        ref = AR.at[s, b, h, x, :, pl.ds(g * 512, 512)]
         return remote(ref, ref, a_s.at[0], a_r.at[b, h], at(0, z, xk(k), y))
 
     def attended_arrival(s, b, h):
@@ -268,7 +281,7 @@
             H[0, b, 1, y, x] = TS[x, b, 1]
             T0[b, x] = TS[x, b, 0]
         for half in (1, 0):
-            for k in range(1, 4):
+            for k in FAR_FIRST:
                 text_copy(half, k).start()
 
     def image_part():
@@ -286,16 +299,16 @@
                     for n in range(2):
                         part = product[:, n * 128 : (n + 1) * 128]
                         IS[b, 2 * pair + n, :, :, zz * 128 : (zz + 1) * 128] = part.reshape(4, 64, 128)
-            for k in range(1, 4):
+            for k in FAR_FIRST:
                 image_copy(b, k).start()
         text_arrival(0)
         for b in range(2):
             image_arrival(b)
             total = IS[b, x].astype(F32)
-            for k in range(1, 4):
+            for k in FAR_FIRST:
                 total = total + IR[b, xk(k)].astype(F32)
             H[0, b, 0, y] = (total.astype(BF).astype(F32) + T0[b].astype(F32)).astype(BF)
-            for k in range(1, 4):
+            for k in FAR_FIRST:
                 hidden_copy(0, b, 0, k).start()
 
     def project(s, b, h):
@@ -326,13 +339,13 @@
 
             @pl.when(n == 2)
             def _():
-                for k in range(1, 4):
+                for k in FAR_FIRST:
                     qkv_copy(s, b, h, k, 0).start()
 
             return 0
 
         lax.fori_loop(0, 6, tile, 0)
-        for k in range(1, 4):
+        for k in FAR_FIRST:
             qkv_copy(s, b, h, k, 1).start()
 
     def attend(s, b, h):
@@ -341,7 +354,7 @@
         def summed(start, size=64):
             rows = slice(start, start + size)
             total = QS[s, b, h, x, rows].astype(F32)
-            for k in range(1, 4):
+            for k in FAR_FIRST:
                 total = total + QR[s, b, h, xk(k), rows].astype(F32)
             return total
 
@@ -374,21 +387,22 @@
             for j in range(4):
                 lanes = (4 * g + j) * 128
                 AR[s, b, h, x, :, lanes : lanes + 128] = mixed[j * 64 : (j + 1) * 64].astype(BF)
-        for k in range(1, 4):
-            attended_copy(s, b, h, k).start()
+            for k in FAR_FIRST:
+                attended_copy(s, b, h, k, g).start()
 
     def update(s, b, h):
         attended_arrival(s, b, h)
 
         def tile(n, _):
-            yd = yk(n + 1)
+            k = jnp.where(n == 0, 2, jnp.where(n == 1, 1, jnp.where(n == 2, 3, 0)))
+            yd = yk(k)
             lanes = pl.ds(pl.multiple_of(yd * 256, 256), 256)
             product = jnp.dot(AR[s, b, h].reshape(256, 1024), WO[s, :, lanes], preferred_element_type=F32)
             OS[s, b, h, yd] = product.astype(BF).reshape(4, 64, 256)
 
             @pl.when(n < 3)
             def _():
-                update_copy(s, b, h, n + 1).start()
+                update_copy(s, b, h, k).start()
 
             return 0
 
@@ -397,20 +411,20 @@
     def renew(s, b, h):
         update_arrival(s, b, h)
         total = OS[s, b, h, y].astype(F32)
-        for k in range(1, 4):
+        for k in FAR_FIRST:
             total = total + OR[s, b, h, yk(k)].astype(F32)
         fresh = (H[s, b, h, y].astype(F32) + total).astype(BF)
 
         @pl.when(s == 0)
         def _():
             H[1, b, h, y] = fresh
-            for k in range(1, 4):
+            for k in FAR_FIRST:
                 hidden_copy(1, b, h, k).start()
 
         @pl.when(s == 1)
         def _():
             FS[b, h] = fresh
-            for k in range(1, 4):
+            for k in FAR_FIRST:
                 final_copy(b, h, k).start()
 
             @pl.when(h == 0)
@@ -436,11 +450,11 @@
         VS[...] = jnp.zeros_like(VS)
         normed_patches()
         PN[x, :, 0] = PNS[x]
-        for k in range(1, 4):
+        for k in FAR_FIRST:
             patch_copy(k).start()
         text_arrival(1)
         for b in range(2):
-            for k in range(1, 4):
+            for k in FAR_FIRST:
                 hidden_copy(0, b, 1, k).start()
         image_part()
 

time: 119 us -> 116 us (0.975)
  Pallas kernels: 117 us -> 115 us
    pallas_call x1, Pallas kernels: 117 us -> 115 us  [shards(): pl.pallas_call(kernel, out_shape=jax.ShapeDtypeStruct((2, 64, 1024), BF),...]
where the time goes in v5:
time: 116 us
  Pallas kernels  115 us (99%)
  local copies, waits for them, and re-layouts  1.67 us (1%)
    pallas_call x1, Pallas kernels, shards(): pl.pallas_call(kernel, out_shape=jax.ShapeDtypeStruct((2, 64, 1024), BF),...  115 us

profile of v5, /device:TPU:1, one launch (start us, length us, event | category | flops | bytes accessed | tf_op | source)
XLA Modules:
  0.0 116.3 jit_solution(6218946184788966592)
XLA Ops:
  0.0 114.6 %decoder.1 = bf16[2,64,1024]{2,1,0:T(8,128)(2,1)} custom-call(bf16[2,128,1024]{2,1,0:T(8,128)(2,1)} %text_in.1, bf16[2,32,3200]{2,1,0:T(8,128)(2,1)} %patches_in.1, s32[2]{0:T(128)} %tokens_in.1, bf16[100,1024]{1,0:T(8,128)(2,1)} %conn_in.1, bf16[1,128,1024]{2,1,0:T(8,128)(2,1)} %wq.1, bf16[1,2,128,256]{3,2,1,0:T(8,128)(2,1)} %wkv.1, ...), custom_call_target="tpu_custom_call" | custom-call | flops 11000000512 | bytes 20000000 | tf_op jit(solution)/shard_map/decoder/pallas_call | solution.py:544
  114.6 1.7 %copy.11 = bf16[2,64,1024]{2,1,0:T(8,128)(2,1)} copy(bf16[2,64,1024]{2,1,0:T(8,128)(2,1)} %decoder.1) | data formatting | bytes 524288

commit v6 on v5

--- a/solution.py
+++ b/solution.py
@@ -19,7 +19,11 @@
     (0, 2), (0, 3), (0, 4), (1, 2), (1, 3), (1, 4), (2, 1), (2, 2), (2, 3), (3, 1), (2, 4),
     (3, 2), (3, 3), (4, 1), (3, 4), (4, 2), (4, 3), (4, 4),
 ]
-PIECES = (((0, 32), (32, 32), (64, 32), (96, 16)), ((0, 32), (32, 32), (64, 32), (96, 32)), ((0, 512), (512, 512)))
+PIECES = (
+    ((0, 16), (16, 16), (32, 32), (64, 16), (80, 16), (96, 16)),
+    ((0, 32), (32, 32), (64, 32), (96, 32)),
+    ((0, 512), (512, 512)),
+)
 WHOLE = (112, 128, 1024)
 
 PROJECT, ATTEND, UPDATE, RENEW = range(4)
@@ -245,7 +249,7 @@
         waits(H.at[s, b, h, pl.ds(0, 3)], h_r.at[b, h]).wait_recv()
 
     def qkv_copy(s, b, h, k, part):
-        rows = pl.ds(0, 384) if part == 0 else pl.ds(384, 400)
+        rows = pl.ds(0, 256) if part == 0 else pl.ds(256, 528)
         return remote(
             QS.at[s, b, h, xk(k), rows], QR.at[s, b, h, x, rows], q_s.at[0], q_r.at[b, h], at(0, z, xk(k), y)
         )
@@ -337,7 +341,7 @@
                 rows = pl.ds(pl.multiple_of((2 * n + i) * 64, 64), 64)
                 QS[s, b, h, :, rows, :] = total[:, i * 128 : (i + 1) * 128].astype(BF).reshape(4, 64, 128)
 
-            @pl.when(n == 2)
+            @pl.when(n == 1)
             def _():
                 for k in FAR_FIRST:
                     qkv_copy(s, b, h, k, 0).start()
@@ -574,7 +578,7 @@
             pltpu.VMEM((4, 2, 64, 256), BF),
             dma((10,)),
             dma((2,)), dma((2,)),
-            dma((5,)), dma((3, 3, 2, 4)),
+            dma((5,)), dma((3, 3, 2, 6)),
             dma((5,)), dma((5,)),
             dma((1,)), dma((2,)),
             dma((1,)), dma((2,)),

time: 116 us -> 116 us (level)
  no operation moved by 1% of the time
where the time goes in v6:
time: 116 us
  Pallas kernels  114 us (98%)
  local copies, waits for them, and re-layouts  1.67 us (1%)
    pallas_call x1, Pallas kernels, shards(): pl.pallas_call(kernel, out_shape=jax.ShapeDtypeStruct((2, 64, 1024), BF),...  114 us

profile of v6, /device:TPU:1, one launch (start us, length us, event | category | flops | bytes accessed | tf_op | source)
XLA Modules:
  0.0 115.7 jit_solution(2870320309567912082)
XLA Ops:
  0.0 114.0 %decoder.1 = bf16[2,64,1024]{2,1,0:T(8,128)(2,1)} custom-call(bf16[2,128,1024]{2,1,0:T(8,128)(2,1)} %text_in.1, bf16[2,32,3200]{2,1,0:T(8,128)(2,1)} %patches_in.1, s32[2]{0:T(128)} %tokens_in.1, bf16[100,1024]{1,0:T(8,128)(2,1)} %conn_in.1, bf16[1,128,1024]{2,1,0:T(8,128)(2,1)} %wq.1, bf16[1,2,128,256]{3,2,1,0:T(8,128)(2,1)} %wkv.1, ...), custom_call_target="tpu_custom_call" | custom-call | flops 11000000512 | bytes 20000000 | tf_op jit(solution)/shard_map/decoder/pallas_call | solution.py:548
  114.0 1.7 %copy.11 = bf16[2,64,1024]{2,1,0:T(8,128)(2,1)} copy(bf16[2,64,1024]{2,1,0:T(8,128)(2,1)} %decoder.1) | data formatting | bytes 524288
